TPU v7x, 32 devices: a whole 2x2x4 slice. The times are simulated.
32 devices in a mesh: shard: 8 (over z, core), ctx: 2 (over x), tp: 2 (over y).
Axes of the slice: x: 2, y: 2, z: 4, core: 2. Of those that a mesh axis runs over, the one named last changes fastest.
Arguments:
- tokens: bfloat16 [16, 2048, 1024], P('shard', 'ctx'), may hold values from -6 to 6
- cotangent: bfloat16 [16, 2048, 1024], P('shard', 'ctx'), may hold values from -6 to 6
- adapter_pick: int32 [16], P('shard'), may hold values from 0 to 7
- positions: int32 [3, 16, 2048], P(None, 'shard', 'ctx'), may hold values from 0 to 15
- first_gain: float32 [1024], replicated, may hold values from 0.1 to 1.9
- first_shift: float32 [1024], replicated, may hold values from -3 to 3
- joined_weight: bfloat16 [1024, 3, 1024], P('shard', None, 'tp'), may hold values from -0.1875 to 0.1875
- joined_bias: float32 [3, 1024], P(None, 'tp'), may hold values from -3 to 3
- output_weight: bfloat16 [1024, 1024], P('tp', 'shard'), may hold values from -0.75 to 0.75
- mixing_exit_offset: float32 [1024], replicated, may hold values from -3 to 3
- second_gain: float32 [1024], replicated, may hold values from 0.1 to 1.9
- second_shift: float32 [1024], replicated, may hold values from -3 to 3
- expand_weight: bfloat16 [1024, 4096], P('shard', 'tp'), may hold values from -0.1875 to 0.1875
- widening_offset: float32 [4096], P('tp'), may hold values from -3 to 3
- reduce_weight: bfloat16 [4096, 1024], P('tp', 'shard'), may hold values from -0.09375 to 0.09375
- shrinking_offset: float32 [1024], replicated, may hold values from -3 to 3
- joined_down: bfloat16 [8, 1024, 16], replicated, may hold values from -0.1875 to 0.1875
- joined_up: bfloat16 [8, 16, 3, 1024], P(None, None, None, 'tp'), may hold values from -1.5 to 1.5
- output_down: bfloat16 [8, 1024, 16], P(None, 'tp'), may hold values from -0.75 to 0.75
- output_up: bfloat16 [8, 16, 1024], replicated, may hold values from -1.5 to 1.5
- expand_down: bfloat16 [8, 1024, 16], replicated, may hold values from -0.1875 to 0.1875
- expand_up: bfloat16 [8, 16, 4096], P(None, None, 'tp'), may hold values from -1.5 to 1.5
- reduce_down: bfloat16 [8, 4096, 16], P(None, 'tp'), may hold values from -0.09375 to 0.09375
- reduce_up: bfloat16 [8, 16, 1024], replicated, may hold values from -1.5 to 1.5
Outputs:
- output: bfloat16 [16, 2048, 1024], P('shard', 'ctx')
- tokens_grad: bfloat16 [16, 2048, 1024], P('shard', ('ctx', 'tp'))
- joined_down_grad: float32 [8, 1024, 16], replicated
- joined_up_grad: float32 [8, 16, 3, 1024], P(None, None, None, 'tp')
- output_down_grad: float32 [8, 1024, 16], P(None, 'tp')
- output_up_grad: float32 [8, 16, 1024], replicated
- expand_down_grad: float32 [8, 1024, 16], replicated
- expand_up_grad: float32 [8, 16, 4096], P(None, None, 'tp')
- reduce_down_grad: float32 [8, 4096, 16], P(None, 'tp')
- reduce_up_grad: float32 [8, 16, 1024], replicated
Inputs may be any that keep to these rules, and one draw needn't show every extreme that they name: `positions`: integer places on a grid of 16 frames by 16 by 16 patches.
All inputs are finite; a program needn't handle non-finite values.
Results may differ from a plain program's by a relative error of at most 0.022.
The roundings to bfloat16 on the way count: a program that leaves them out, or rounds other values in their place, can miss the bound.
Values may be sent and summed in bfloat16 or wider, within the bound.
A program may use at most 448 MiB of HBM per device.

v0:
```python
import functools
import math

import jax
import jax.numpy as jnp
import ml_dtypes
import numpy as np
from jax import lax
from jax.experimental import pallas as pl
from jax.experimental.pallas import tpu as pltpu
from jax.sharding import PartitionSpec as P

eps_norm = 1e-06
score_scale = 0.125


def rope_tables(places):
    band = jnp.arange(10, dtype=jnp.float32)
    rates = jnp.exp(band * (-math.log(10000.0) / 10.0))
    angle = places.astype(jnp.float32)[..., None] * rates
    cos_parts = []
    sin_parts = []
    for band_index in range(3):
        cosine = jnp.cos(angle[band_index])
        sine = jnp.sin(angle[band_index])
        cos_parts = cos_parts + [cosine, cosine]
        sin_parts = sin_parts + [-sine, sine]
    rest_shape = angle.shape[1:-1] + (4,)
    cos_parts.append(jnp.ones(rest_shape, jnp.float32))
    sin_parts.append(jnp.zeros(rest_shape, jnp.float32))
    return (jnp.concatenate(cos_parts, -1), jnp.concatenate(sin_parts, -1))


def swap_pairs(values):
    leading = values.shape[:-1]
    turned = values[..., :60].reshape(leading + (3, 2, 10))[..., ::-1, :].reshape(leading + (60,))
    return jnp.concatenate([turned, values[..., 60:]], -1)


def rotate(values, cosine, sine):
    return values * cosine[..., None, :] + swap_pairs(values) * sine[..., None, :]


def rotate_back(grads, cosine, sine):
    return grads * cosine[..., None, :] + swap_pairs(grads * sine[..., None, :])


def norm_forward(values, gain, shift):
    centred = values - jnp.mean(values, -1, keepdims=True)
    inverse = lax.rsqrt(jnp.mean(centred * centred, -1, keepdims=True) + eps_norm)
    scaled = centred * inverse
    return (scaled * gain + shift, scaled, inverse)


def norm_back(grads, scaled, inverse, gain):
    weighted = grads * gain
    return inverse * (
        weighted
        - jnp.mean(weighted, -1, keepdims=True)
        - scaled * jnp.mean(weighted * scaled, -1, keepdims=True)
    )


def select_factor(choose, table):
    return jnp.einsum("ca,a...->c...", choose, table, preferred_element_type=jnp.float32).astype(
        jnp.bfloat16
    )


def gelu_exact(values):
    return jax.nn.gelu(values, approximate=False)


def matrix_product(form, left, right):
    return jnp.einsum(form, left, right, preferred_element_type=jnp.float32)


def general_shards(
    tokens,
    cotangent,
    adapter_pick,
    positions,
    first_gain,
    first_shift,
    joined_weight,
    joined_bias,
    output_weight,
    mixing_exit_offset,
    second_gain,
    second_shift,
    expand_weight,
    widening_offset,
    reduce_weight,
    shrinking_offset,
    joined_down,
    joined_up,
    output_down,
    output_up,
    expand_down,
    expand_up,
    reduce_down,
    reduce_up,
):
    whole_joined, whole_output, whole_expand, whole_reduce = (
        lax.all_gather(joined_weight, "shard", axis=0, tiled=True),
        lax.all_gather(output_weight, "shard", axis=1, tiled=True),
        lax.all_gather(expand_weight, "shard", axis=0, tiled=True),
        lax.all_gather(reduce_weight, "shard", axis=1, tiled=True),
    )
    clip_count, local_len, width = tokens.shape
    local_width = whole_joined.shape[2]
    head_count = local_width // 64
    choose = (
        adapter_pick[:, None] == jnp.arange(joined_down.shape[0], dtype=jnp.int32)[None, :]
    ).astype(jnp.bfloat16)
    select_joined_down = select_factor(choose, joined_down)
    select_joined_up = select_factor(choose, joined_up)
    select_output_down = select_factor(choose, output_down)
    select_output_up = select_factor(choose, output_up)
    select_expand_down = select_factor(choose, expand_down)
    select_expand_up = select_factor(choose, expand_up)
    select_reduce_down = select_factor(choose, reduce_down)
    select_reduce_up = select_factor(choose, reduce_up)
    cosine, sine = rope_tables(positions)
    block_arguments = tokens.astype(jnp.float32)
    norm_one, scaled_one, inverse_one = norm_forward(block_arguments, first_gain, first_shift)
    initial_standardized = norm_one.astype(jnp.bfloat16)
    initial_slim_derivative = matrix_product(
        "zgh,zhe->zge", initial_standardized, select_joined_down
    ).astype(jnp.bfloat16)
    mapped_vectors = (
        matrix_product("cld,dje->clje", initial_standardized, whole_joined)
        + joined_bias
        + matrix_product("uip,upqg->uiqg", initial_slim_derivative, select_joined_up)
    )
    head_shape = (clip_count, local_len, head_count, 64)
    query = rotate(mapped_vectors[:, :, 0].reshape(head_shape), cosine, sine).astype(jnp.bfloat16)
    keys = rotate(mapped_vectors[:, :, 1].reshape(head_shape), cosine, sine).astype(jnp.bfloat16)
    values = mapped_vectors[:, :, 2].reshape(head_shape).astype(jnp.bfloat16)
    stats_shape = (clip_count, head_count, local_len)
    run_max = jnp.full(stats_shape, -1e30, jnp.float32)
    key_part = lax.all_gather(keys, "ctx", axis=1, tiled=True)
    value_part = lax.all_gather(values, "ctx", axis=1, tiled=True)
    scores = matrix_product("cqhd,ckhd->chqk", query, key_part) * score_scale
    new_max = jnp.maximum(run_max, jnp.max(scores, -1))
    weights = jnp.exp(scores - new_max[..., None])
    run_total = jnp.sum(weights, -1)
    update = matrix_product("chqk,ckhd->cqhd", weights.astype(jnp.bfloat16), value_part)
    accum = update
    run_max, run_total, accum = (new_max, run_total, accum)
    log_total = run_max + jnp.log(run_total)
    attended_full = accum / jnp.transpose(run_total, (0, 2, 1))[..., None]
    mixing_outcome = attended_full.reshape(clip_count, local_len, local_width).astype(jnp.bfloat16)
    out_part = matrix_product("cle,ed->cld", mixing_outcome, whole_output)
    rank_partial = matrix_product("fig,fgt->fit", mixing_outcome, select_output_down)
    output_total, rank_sum = (
        lax.psum(out_part.astype(jnp.bfloat16), "tp").astype(jnp.float32),
        lax.psum(rank_partial.astype(jnp.bfloat16), "tp").astype(jnp.float32),
    )
    middle_slim_derivative = rank_sum.astype(jnp.bfloat16)
    first_hidden = (
        block_arguments
        + output_total
        + mixing_exit_offset
        + matrix_product("wnk,wke->wne", middle_slim_derivative, select_output_up)
    )
    norm_two, scaled_two, inverse_two = norm_forward(first_hidden, second_gain, second_shift)
    latter_standardized = norm_two.astype(jnp.bfloat16)
    penultimate_slim_derivative = matrix_product(
        "zgh,zhe->zge", latter_standardized, select_expand_down
    ).astype(jnp.bfloat16)
    skip_stream_vectors = (
        matrix_product("cld,df->clf", latter_standardized, whole_expand)
        + widening_offset
        + matrix_product("uqz,uze->uqe", penultimate_slim_derivative, select_expand_up)
    )
    activity, gelu_pull = jax.vjp(gelu_exact, skip_stream_vectors)
    gaussian_error_unit = activity.astype(jnp.bfloat16)
    mlp_part = matrix_product("clf,fd->cld", gaussian_error_unit, whole_reduce)
    fourth_rank_partial = matrix_product("xpv,xvy->xpy", gaussian_error_unit, select_reduce_down)
    feedforward_sum, rank_four_sum = (
        lax.psum(mlp_part.astype(jnp.bfloat16), "tp").astype(jnp.float32),
        lax.psum(fourth_rank_partial.astype(jnp.bfloat16), "tp").astype(jnp.float32),
    )
    closing_slim_derivative = rank_four_sum.astype(jnp.bfloat16)
    output = (
        first_hidden
        + feedforward_sum
        + shrinking_offset
        + matrix_product("wnk,wke->wne", closing_slim_derivative, select_reduce_up)
    ).astype(jnp.bfloat16)
    back_joined, back_output, back_expand, back_reduce = (
        lax.all_gather(joined_weight, "shard", axis=0, tiled=True),
        lax.all_gather(output_weight, "shard", axis=1, tiled=True),
        lax.all_gather(expand_weight, "shard", axis=0, tiled=True),
        lax.all_gather(reduce_weight, "shard", axis=1, tiled=True),
    )
    reduce_up_term = matrix_product("vkn,vkm->vnm", closing_slim_derivative, cotangent)
    gradient_fourth = matrix_product("abj,awj->abw", cotangent, select_reduce_up).astype(
        jnp.bfloat16
    )
    reduce_down_term = matrix_product("mpg,mpu->mgu", gaussian_error_unit, gradient_fourth)
    grad_active = matrix_product("cld,fd->clf", cotangent, back_reduce) + matrix_product(
        "gez,guz->geu", gradient_fourth, select_reduce_down
    )
    residual_gradient = gelu_pull(grad_active)[0].astype(jnp.bfloat16)
    expand_up_term = matrix_product("jge,jgn->jen", penultimate_slim_derivative, residual_gradient)
    grad_norm_part = matrix_product("clf,df->cld", residual_gradient, back_expand)
    third_gradient_part = matrix_product("aik,adk->aid", residual_gradient, select_expand_up)
    norm_gradient_sum, grad_three_sum = (
        lax.psum(grad_norm_part.astype(jnp.bfloat16), "tp").astype(jnp.float32),
        lax.psum(third_gradient_part.astype(jnp.bfloat16), "tp").astype(jnp.float32),
    )
    gradient_third = grad_three_sum.astype(jnp.bfloat16)
    expand_down_term = matrix_product("kgt,kgh->kth", latter_standardized, gradient_third)
    second_norm_gradient = norm_gradient_sum + matrix_product(
        "jqt,jit->jqi", gradient_third, select_expand_down
    )
    grad_hidden = cotangent.astype(jnp.float32) + norm_back(
        second_norm_gradient, scaled_two, inverse_two, second_gain
    )
    branch_gradient = grad_hidden.astype(jnp.bfloat16)
    output_up_term = matrix_product("vkn,vkm->vnm", middle_slim_derivative, branch_gradient)
    gradient_second = matrix_product("abj,awj->abw", branch_gradient, select_output_up).astype(
        jnp.bfloat16
    )
    output_down_term = matrix_product("nua,nui->nai", mixing_outcome, gradient_second)
    grad_attended = (
        (
            matrix_product("cld,ed->cle", branch_gradient, back_output)
            + matrix_product("gsq,ghq->gsh", gradient_second, select_output_down)
        )
        .astype(jnp.bfloat16)
        .reshape(head_shape)
    )
    key_whole, value_whole = (
        lax.all_gather(keys, "ctx", axis=1, tiled=True),
        lax.all_gather(values, "ctx", axis=1, tiled=True),
    )
    flat_shape = (clip_count, local_len, local_width)

    def clip_back(items):
        query_clip, key_clip, value_clip, grad_clip, total_clip = items
        scores = matrix_product("qhd,khd->hqk", query_clip, key_clip) * score_scale
        probs = jnp.exp(scores - total_clip[..., None])
        grad_probs = matrix_product("qhd,khd->hqk", grad_clip, value_clip)
        middle = jnp.sum(probs * grad_probs, -1, keepdims=True)
        grad_scores = (probs * (grad_probs - middle)).astype(jnp.bfloat16)
        grad_query = matrix_product("hqk,khd->qhd", grad_scores, key_clip) * score_scale
        grad_key = matrix_product("hqk,qhd->khd", grad_scores, query_clip) * score_scale
        grad_value = matrix_product("hqk,qhd->khd", probs.astype(jnp.bfloat16), grad_clip)
        return (grad_query, grad_key, grad_value)

    grad_query, key_terms, value_terms = lax.map(
        clip_back, (query, key_whole, value_whole, grad_attended, log_total)
    )
    full_len = key_whole.shape[1]
    key_sum, value_sum = (
        lax.psum_scatter(
            key_terms.reshape(clip_count, full_len, local_width).astype(jnp.bfloat16),
            "ctx",
            scatter_dimension=1,
            tiled=True,
        ).astype(jnp.float32),
        lax.psum_scatter(
            value_terms.reshape(clip_count, full_len, local_width).astype(jnp.bfloat16),
            "ctx",
            scatter_dimension=1,
            tiled=True,
        ).astype(jnp.float32),
    )
    query_key_value_gradient = jnp.stack(
        [
            rotate_back(grad_query, cosine, sine).reshape(flat_shape),
            rotate_back(key_sum.reshape(head_shape), cosine, sine).reshape(flat_shape),
            value_sum,
        ],
        axis=2,
    ).astype(jnp.bfloat16)
    joined_up_term = matrix_product(
        "pvh,pvfo->phfo", initial_slim_derivative, query_key_value_gradient
    )
    first_gradient_part = matrix_product(
        "kxsd,ktsd->kxt", query_key_value_gradient, select_joined_up
    )
    grad_norm_one_part = matrix_product("clje,dje->cld", query_key_value_gradient, back_joined)
    gradient_first = lax.psum(first_gradient_part.astype(jnp.bfloat16), "tp")
    grad_norm_share = lax.psum_scatter(
        grad_norm_one_part.astype(jnp.bfloat16), "tp", scatter_dimension=1, tiled=True
    ).astype(jnp.float32)
    joined_down_term = matrix_product("kgt,kgh->kth", initial_standardized, gradient_first)
    half_len = grad_norm_share.shape[1]
    begin = lax.axis_index("tp") * half_len

    def shared_rows(array):
        return lax.dynamic_slice_in_dim(array, begin, half_len, 1)

    grad_norm_one = grad_norm_share + matrix_product(
        "jqt,jit->jqi", shared_rows(gradient_first), select_joined_down
    )
    tokens_grad = (
        shared_rows(grad_hidden)
        + norm_back(grad_norm_one, shared_rows(scaled_one), shared_rows(inverse_one), first_gain)
    ).astype(jnp.bfloat16)
    choose_full = choose.astype(jnp.float32)

    def by_adapter(term):
        return jnp.einsum(
            "ca,c...->a...",
            choose_full,
            term,
            precision=lax.Precision.HIGHEST,
            preferred_element_type=jnp.float32,
        )

    summed = lax.psum(
        (
            by_adapter(joined_down_term),
            by_adapter(joined_up_term),
            by_adapter(output_down_term),
            by_adapter(output_up_term),
            by_adapter(expand_down_term),
            by_adapter(expand_up_term),
            by_adapter(reduce_down_term),
            by_adapter(reduce_up_term),
        ),
        ("shard", "ctx"),
    )
    return (
        output,
        tokens_grad,
        summed[0],
        summed[1],
        summed[2],
        summed[3],
        summed[4],
        summed[5],
        summed[6],
        summed[7],
    )


B16 = jnp.bfloat16
F32 = jnp.float32
VMEM_LIMIT = 60 * 2**20
exp_scale = score_scale * math.log2(math.e)


def dot(left, right, left_dim=1, right_dim=0):
    return lax.dot_general(
        left, right, (((left_dim,), (right_dim,)), ((), ())), preferred_element_type=F32
    )


def params():
    return pltpu.CompilerParams(vmem_limit_bytes=VMEM_LIMIT)


def low_lanes():
    return lax.broadcasted_iota(jnp.int32, (1, 128), 1) < 64


def partner(values):
    lane = lax.broadcasted_iota(jnp.int32, (1, 128), 1) % 64 % 20
    return jnp.where(lane < 10, pltpu.roll(values, 118, 1), pltpu.roll(values, 10, 1))


def row_norm(values):
    centred = values - jnp.mean(values, -1, keepdims=True)
    inverse = lax.rsqrt(jnp.mean(centred * centred, -1, keepdims=True) + eps_norm)
    return centred * inverse, inverse


def back_norm(weighted, scaled, inverse):
    return inverse * (
        weighted
        - jnp.mean(weighted, -1, keepdims=True)
        - scaled * jnp.mean(weighted * scaled, -1, keepdims=True)
    )


MESH = pl.DeviceIdType.MESH
HIDDEN_BLOCK = 512
(UP_SENT, DOWN_SENT, Z_CAME, TP_SENT, TP_CAME, OWN_SENT, OWN_CAME, NEXT_SENT, NEXT_CAME) = range(9)


class Place:
    def __init__(self, planes):
        self.planes = planes
        self.shard = lax.axis_index("shard")
        self.z = self.shard // 2
        self.core = self.shard % 2
        self.ctx = lax.axis_index("ctx")
        self.tp = lax.axis_index("tp")
        self.has_up = self.z < planes - 1
        self.has_down = self.z > 0
        self.crosses = self.core != self.ctx
        self.up = {"shard": self.shard + 2}
        self.down = {"shard": self.shard - 2}
        self.next_tp = {"tp": 1 - self.tp}
        self.next_core = {"shard": 2 * self.z + 1 - self.core}
        self.turned = {"shard": 2 * self.z + self.ctx, "ctx": self.core}

    def greet(self, planes_too, turned, ctx_too=False, flipped=False):
        barrier = pltpu.get_barrier_semaphore()
        count = 2

        def signal(device):
            pl.semaphore_signal(barrier, inc=1, device_id=device, device_id_type=MESH)

        signal(self.next_tp)
        signal(self.next_core)
        if planes_too:
            pl.when(self.has_up)(lambda: signal(self.up))
            pl.when(self.has_down)(lambda: signal(self.down))
            count = count + self.has_up.astype(jnp.int32) + self.has_down.astype(jnp.int32)
        if turned:
            pl.when(self.crosses)(lambda: signal(self.turned))
            count = count + self.crosses.astype(jnp.int32)
        if ctx_too:
            signal({"ctx": 1 - self.ctx})
            count = count + 1
        if flipped:
            flip = dict(self.turned)
            flip["tp"] = 1 - self.tp
            pl.when(self.crosses)(lambda: signal(flip))
            count = count + self.crosses.astype(jnp.int32)
        pl.semaphore_wait(barrier, count)


class Flow:
    def __init__(self, at, own, slot, sems, kinds=tuple(range(9))):
        self.at, self.own, self.slot = at, own, slot
        self.sems = {kind: sems[i] for i, kind in enumerate(kinds)}

    def copy(self, kind, plane, own=False):
        at = self.at
        half = 1 - at.tp if kind == NEXT_SENT else at.tp
        piece = self.slot(2 * plane + at.core, half)
        device, came = {
            UP_SENT: (at.up, Z_CAME),
            DOWN_SENT: (at.down, Z_CAME),
            TP_SENT: (at.next_tp, TP_CAME),
            OWN_SENT: (at.next_core, OWN_CAME),
            NEXT_SENT: (at.next_core, NEXT_CAME),
        }[kind]
        return pltpu.make_async_remote_copy(
            src_ref=self.own if own else piece,
            dst_ref=piece,
            send_sem=self.sems[kind].at[plane],
            recv_sem=self.sems[came].at[plane],
            device_id=device,
            device_id_type=MESH,
        )

    def came(self, kind, plane):
        at = self.at
        shard = 2 * plane + (at.core if kind in (Z_CAME, TP_CAME) else 1 - at.core)
        half = at.tp if kind in (Z_CAME, OWN_CAME) else 1 - at.tp
        piece = self.slot(shard, half)
        return pltpu.make_async_remote_copy(
            src_ref=piece, dst_ref=piece, send_sem=self.sems[kind].at[plane],
            recv_sem=self.sems[kind].at[plane], device_id=at.next_core, device_id_type=MESH,
        )

    def pieces(self, distance):
        at = self.at
        if distance == 0:
            return [(None, at.z, True, True)]
        return [
            (at.z >= distance, at.z - distance, True, False),
            (at.z < at.planes - distance, at.z + distance, False, True),
        ]

    def each(self, distance, act):
        for there, plane, below, above in self.pieces(distance):
            if there is None:
                act(plane, below, above)
            else:
                pl.when(there)(functools.partial(act, plane, below, above))

    def pass_on(self, distance, z=False, tp=False, core=False, fresh=None, wait=False):
        own = (distance == 0) if fresh is None else fresh

        def act(plane, below, above):
            if wait:
                self.came(Z_CAME, plane).wait_recv()
            if z:
                if below:
                    pl.when(self.at.has_up)(lambda: self.copy(UP_SENT, plane, own).start())
                if above:
                    pl.when(self.at.has_down)(lambda: self.copy(DOWN_SENT, plane, own).start())
            if tp:
                self.copy(TP_SENT, plane, own).start()
            if core:
                self.copy(OWN_SENT, plane, own).start()

        self.each(distance, act)

    def sent(self, distance, z=False, tp=False, core=False):
        def act(plane, below, above):
            if z:
                if below:
                    pl.when(self.at.has_up)(lambda: self.copy(UP_SENT, plane).wait_send())
                if above:
                    pl.when(self.at.has_down)(lambda: self.copy(DOWN_SENT, plane).wait_send())
            if tp:
                self.copy(TP_SENT, plane).wait_send()
            if core:
                self.copy(OWN_SENT, plane).wait_send()

        self.each(distance, act)

    def wait(self, kind, distance):
        self.each(distance, lambda plane, below, above: self.came(kind, plane).wait_recv())

    def pass_next(self, distance, wait=True):
        def act(plane, below, above):
            if wait:
                self.came(TP_CAME, plane).wait_recv()
            self.copy(NEXT_SENT, plane).start()

        self.each(distance, act)

    def sent_next(self, distance):
        self.each(distance, lambda plane, below, above: self.copy(NEXT_SENT, plane).wait_send())


ALONG_Z = (UP_SENT, DOWN_SENT, Z_CAME)
TO_TP = (TP_SENT, TP_CAME)
TO_CORE = (OWN_SENT, OWN_CAME)
TO_NEXT = (NEXT_SENT, NEXT_CAME)
EVERY = ALONG_Z + TO_TP + TO_CORE + TO_NEXT


class Rows:
    def __init__(self, sems):
        self.sems, self.used = sems, 0

    def take(self, kinds):
        rows = [self.sems.at[self.used + i] for i in range(len(kinds))]
        self.used += len(kinds)
        return rows


def block_flows(at, own_e, own_r, full_e, full_r, rows, kinds):
    flows = []
    for block, needs in enumerate(kinds):
        span = pl.ds(block * HIDDEN_BLOCK, HIDDEN_BLOCK)
        flows.append(
            [
                Flow(
                    at, None if own_e is None else own_e.at[:, span],
                    lambda s, h, span=span: full_e.at[s, h, :, span], rows.take(needs), needs,
                ),
                Flow(
                    at, None if own_r is None else own_r.at[span, :],
                    lambda s, h, span=span: full_r.at[s, h, span, :], rows.take(needs), needs,
                ),
            ]
        )
    return flows


def count_rows(first, kinds):
    return len(first) + 2 * sum(len(needs) for needs in kinds)


PROJECT_KINDS = (ALONG_Z, ALONG_Z)
ATTEND_KINDS = (EVERY, ALONG_Z + TO_TP + TO_CORE, ALONG_Z + TO_CORE, ALONG_Z)
MIDDLE_KINDS = ((), TO_TP + TO_NEXT, TO_TP + TO_NEXT, EVERY)


def turned_copy(at, source, target, sems):
    return pltpu.make_async_remote_copy(
        src_ref=source, dst_ref=target, send_sem=sems.at[0], recv_sem=sems.at[1],
        device_id=at.turned, device_id_type=MESH,
    )


class Spread:
    def __init__(self, at, split, full, tag, sums, give, take, pass_tp, stack, beyond, sems):
        self.at, self.split, self.full, self.tag, self.sums = at, split, full, tag, sums
        self.give, self.take, self.pass_tp, self.stack, self.beyond, self.sems = (
            give, take, pass_tp, stack, beyond, sems,
        )
        self.ranks = give.shape[0]
        self.width = split.shape[2]
        self.rest = full.shape[1]

    def remote(self, source, target, index, device):
        return pltpu.make_async_remote_copy(
            src_ref=source, dst_ref=target, send_sem=self.sems.at[0, index], recv_sem=self.sems.at[1, index],
            device_id=device, device_id_type=MESH,
        )

    def between_cores(self):
        return self.remote(self.give, self.take, 0, self.at.next_core)

    def to_tp(self):
        return self.remote(self.pass_tp, self.stack.at[self.at.z, 1], 1, self.at.next_tp)

    def to_ctx(self):
        plane = self.stack.at[self.at.z]
        return self.remote(plane.at[pl.ds(0, 2)], plane.at[pl.ds(2, 2)], 2, {"ctx": 1 - self.at.ctx})

    def along(self, up, plane):
        piece = self.stack.at[plane]
        return pltpu.make_async_remote_copy(
            src_ref=piece, dst_ref=piece, send_sem=self.sems.at[2 + up, plane], recv_sem=self.sems.at[4, plane],
            device_id=self.at.up if up else self.at.down, device_id_type=MESH,
        )

    def over(self, plane):
        return pltpu.make_async_remote_copy(
            src_ref=self.stack.at[plane], dst_ref=self.beyond.at[plane],
            send_sem=self.sems.at[5, plane], recv_sem=self.sems.at[6, plane],
            device_id=self.at.next_core, device_id_type=MESH,
        )

    def rows(self, core):
        return pl.ds(pl.multiple_of(core * self.ranks, self.ranks), self.ranks)

    def start(self):
        theirs = self.rows(1 - self.at.core)
        for half in range(2):
            self.give[:, half * self.width : (half + 1) * self.width] = self.split[half, theirs, :].astype(B16)
        self.give[:, 2 * self.width :] = self.full[theirs, :].astype(B16)
        self.between_cores().start()

    def second(self):
        at, width, rest = self.at, self.width, self.rest
        self.between_cores().wait_recv()
        mine = self.rows(at.core)
        for half, target in ((at.tp, self.stack.at[at.z, 0]), (1 - at.tp, self.pass_tp)):
            span = pl.ds(pl.multiple_of(half * width, 128), width)
            target[:, 0:width] = (self.split[half, mine, :] + self.take[:, span].astype(F32)).astype(B16)
            target[:, width : width + rest] = (
                self.full[mine, :] + self.take[:, 2 * width :].astype(F32)
            ).astype(B16)
            target[:, width + rest :] = self.tag
        self.to_tp().start()

    def third(self):
        self.to_tp().wait_recv()
        self.to_ctx().start()

    def both_ways(self, act_up, act_down, distance):
        at = self.at
        if distance == 0:
            pl.when(at.has_up)(functools.partial(act_up, at.z))
            pl.when(at.has_down)(functools.partial(act_down, at.z))
        else:
            pl.when((at.z >= distance) & at.has_up)(functools.partial(act_up, at.z - distance))
            pl.when((at.z < at.planes - distance) & at.has_down)(functools.partial(act_down, at.z + distance))

    def came(self, distance, act):
        at = self.at
        pl.when(at.z >= distance)(functools.partial(act, at.z - distance))
        pl.when(at.z < at.planes - distance)(functools.partial(act, at.z + distance))

    def planes(self, distance):
        if distance == 0:
            self.to_ctx().wait_recv()
        else:
            self.came(distance, lambda plane: self.along(1, plane).wait_recv())
        if distance < self.at.planes - 1:
            self.both_ways(
                lambda plane: self.along(1, plane).start(), lambda plane: self.along(0, plane).start(), distance
            )
        if distance == 0:
            self.over(self.at.z).start()
        else:
            self.came(distance, lambda plane: self.over(plane).start())

    def finish(self):
        at = self.at
        for plane in range(at.planes):
            self.over(plane).wait_recv()
        keep = self.width + self.rest
        adapters, ranks = self.sums.shape[0], self.ranks
        terms = at.planes * 4 * ranks
        lane = lax.broadcasted_iota(jnp.int32, (terms, 128), 1)
        rank_of = lax.broadcasted_iota(jnp.int32, (terms, 128), 0) % ranks
        for source, core in ((self.stack, at.core), (self.beyond, 1 - at.core)):
            tags = source[:, :, :, keep:].reshape(terms, 128).astype(F32)
            picks = (tags == (lane // ranks).astype(F32)) & (lane % ranks == rank_of)
            choose = jnp.where(picks, 1.0, 0.0).astype(B16)
            for begin in range(0, keep, 512):
                span = pl.ds(begin, min(512, keep - begin))
                total = dot(choose, source[:, :, :, span].reshape(terms, -1), 0, 0)
                for adapter in range(adapters):
                    self.sums[adapter, self.rows(core), span] = total[adapter * ranks : (adapter + 1) * ranks]

    def sent(self):
        self.between_cores().wait_send()
        self.to_tp().wait_send()
        self.to_ctx().wait_send()
        for distance in range(self.at.planes - 1):
            self.both_ways(
                lambda plane: self.along(1, plane).wait_send(),
                lambda plane: self.along(0, plane).wait_send(),
                distance,
            )
        for plane in range(self.at.planes):
            self.over(plane).wait_send()

    @staticmethod
    def scratch(planes, ranks, width, rest):
        wide = width + rest + 128
        return [
            pltpu.VMEM((ranks, 2 * width + rest), B16),
            pltpu.VMEM((ranks, 2 * width + rest), B16),
            pltpu.VMEM((ranks, wide), B16),
            pltpu.VMEM((planes, 4, ranks, wide), B16),
            pltpu.VMEM((planes, 4, ranks, wide), B16),
            pltpu.SemaphoreType.DMA((7, max(planes, 4))),
        ]


ROWS = 256


def project_body(
    planes, blocks,
    tokens_ref, pick_ref, places_ref, bias_ref, wide_ref,
    tab_jd, tab_ed, tab_ou, tab_ru, tab_ju, tab_od, tab_eu, tab_rd,
    w_ref, own_o, own_e, own_r, gain_ref, shift_ref, rates_ref,
    x_out, factors_out, shared_out, offsets_out, w_out, full_o, full_e, full_r,
    q_out, k_out, v_out, xn_out, u_out, cos_out, sin_out,
    spots_ref, offsets_ref, factors_ref, factors_next, shared_ref,
    vm_jd, vm_ed, vm_ou, vm_ru, vm_ju, vm_od, vm_eu, vm_rd,
    x_vm, w_vm, acc, stage, spots_all, factors_vm, offsets_vm, jd_vm,
    w_sems, flow_sems, x_sems, spot_sems, factor_sems, shared_sems, offset_sems, local_sems, out_sems, move_sems, table_sems,
):
    at = Place(planes)
    rows_all, width = x_vm.shape
    depth, half = w_ref.shape[1:]
    at.greet(True, True)
    chunks = rows_all // ROWS
    parts = [
        Flow(
            at, w_ref.at[part], lambda s, h, part=part: w_out.at[s, h, part],
            [w_sems.at[part, kind] for kind in range(9)],
        )
        for part in range(3)
    ]
    taken = Rows(flow_sems)
    flow_o = Flow(at, own_o, lambda s, h: full_o.at[s, h], taken.take(ALONG_Z), ALONG_Z)
    flows = block_flows(at, own_e, own_r, full_e, full_r, taken, PROJECT_KINDS)
    ahead = [flow_o] + flows[0] + flows[1]
    holds = at.core == at.ctx

    def local(source, target, index):
        return pltpu.make_async_copy(source, target, local_sems.at[index])

    for flow in parts:
        flow.pass_on(0, z=True, tp=True)
    tables_in = [
        pltpu.make_async_copy(source, target, table_sems.at[i])
        for i, (source, target) in enumerate(
            (
                (tab_jd, vm_jd), (tab_ed, vm_ed), (tab_ou, vm_ou), (tab_ru, vm_ru),
                (tab_ju, vm_ju), (tab_od, vm_od), (tab_eu, vm_eu), (tab_rd, vm_rd),
            )
        )
    ]
    for table in tables_in:
        table.start()
    place_rows = [places_ref[band, pl.ds(at.tp, 1), :].astype(F32) for band in range(3)]
    spots_ref[...] = jnp.concatenate(
        place_rows * 3 + [jnp.zeros((spots_ref.shape[0] - 9, rows_all), F32)], axis=0
    ).astype(B16)
    for part in range(3):
        offsets_ref[:, part * half : (part + 1) * half] = bias_ref[part : part + 1, :]
    offsets_ref[:, 3 * half :] = wide_ref[...]

    def x_chunk(i):
        span = pl.ds(i * ROWS, ROWS)
        return turned_copy(at, tokens_ref.at[at.tp, span], x_vm.at[span], x_sems.at[i])

    spot_copy = turned_copy(at, spots_ref, spots_all.at[0], spot_sems.at[0])

    @pl.when(at.crosses)
    def _():
        spot_copy.start()
        for i in range(chunks):
            x_chunk(i).start()

    @pl.when(holds)
    def _():
        spots_all[0] = spots_ref[...]
        for i in range(chunks):
            span = pl.ds(i * ROWS, ROWS)
            local(tokens_ref.at[at.tp, span], x_vm.at[span], 1 + i).start()

    for flow in parts:
        flow.pass_on(0, core=True)

    def remote(source, target, sems, device):
        return pltpu.make_async_remote_copy(
            src_ref=source, dst_ref=target, send_sem=sems.at[0], recv_sem=sems.at[1],
            device_id=device, device_id_type=MESH,
        )

    offset_copy = remote(offsets_ref, offsets_out.at[at.tp], offset_sems, at.next_tp)
    offset_came = remote(offsets_ref, offsets_out.at[1 - at.tp], offset_sems, at.next_tp)
    offset_copy.start()
    local(offsets_ref, offsets_out.at[at.tp], 1 + chunks).start()
    next_copy = remote(factors_next, factors_out.at[at.tp], factor_sems.at[0], at.next_tp)
    next_came = remote(factors_next, factors_out.at[1 - at.tp], factor_sems.at[0], at.next_tp)
    own_factors = remote(factors_ref, factors_out.at[at.tp], factor_sems.at[1], at.next_core)
    shared_copy = remote(shared_ref, shared_out, shared_sems, at.next_core)
    next_factors = remote(factors_out.at[1 - at.tp], factors_out.at[1 - at.tp], factor_sems.at[2], at.next_core)

    local(w_ref, w_out.at[at.shard, at.tp], 4 + chunks).start()
    local(own_o, full_o.at[at.shard, at.tp], 5 + chunks).start()
    local(own_e, full_e.at[at.shard, at.tp], 6 + chunks).start()
    local(own_r, full_r.at[at.shard, at.tp], 7 + chunks).start()

    @pl.when(at.crosses)
    def _():
        spot_copy.wait_recv()

    spot_next = remote(spots_all.at[0], spots_all.at[1], spot_sems.at[1], at.next_core)
    spot_next.start()

    lane = lax.broadcasted_iota(jnp.int32, (1, 128), 1) % 64
    turned = lane < 60
    early = lane % 20 < 10

    def tables(part):
        def body(i, carry):
            span = pl.ds(pl.multiple_of(i * ROWS, ROWS), ROWS)
            angle = dot(spots_all[part, :, span], rates_ref[...], 0, 0)
            out = pl.ds(pl.multiple_of(part * rows_all + i * ROWS, ROWS), ROWS)
            cos_out[out, :] = jnp.where(turned, jnp.cos(angle), 1.0)
            sine = jnp.sin(angle)
            sin_out[out, :] = jnp.where(turned, jnp.where(early, -sine, sine), 0.0)
            return carry

        lax.fori_loop(0, chunks, body, 0)

    tables(0)

    for table in tables_in:
        table.wait()

    def chosen(table, pick):
        return sum(
            table[i].astype(F32) * jnp.where(pick == i, 1.0, 0.0) for i in range(table.shape[0])
        ).astype(B16)

    picks = (pick_ref[0], pick_ref[1])
    pick = jnp.where(at.tp == 0, picks[0], picks[1])
    for target, which in ((factors_ref, pick), (factors_next, picks[0] + picks[1] - pick)):
        ju = chosen(vm_ju, which)
        for part in range(3):
            target[:, part * half : (part + 1) * half] = ju[part]
        begin = 3 * half
        for table in (vm_od, vm_eu, vm_rd):
            target[:, begin : begin + table.shape[2]] = chosen(table, which)
            begin += table.shape[2]
    for i, table in enumerate((vm_jd, vm_ed, vm_ou, vm_ru)):
        shared_ref[:, i * width : (i + 1) * width] = chosen(table, pick)
    shared_ref[:, 4 * width :] = jnp.full((shared_ref.shape[0], 128), pick.astype(F32)).astype(B16)

    @pl.when(holds)
    def _():
        next_copy.start()
        own_factors.start()
        shared_copy.start()
        local(factors_ref, factors_out.at[at.tp], 2 + chunks).start()
        local(shared_ref, shared_out, 3 + chunks).start()

    for flow in parts:
        flow.pass_on(1, z=True, tp=True, core=True, wait=True)
    spot_next.wait()
    tables(1)

    @pl.when(holds)
    def _():
        next_came.wait_recv()
        next_factors.start()

    for flow in parts:
        flow.pass_on(2, z=True, tp=True, core=True, wait=True)

    @pl.when(holds)
    def _():
        local(factors_ref, factors_out.at[at.tp], 2 + chunks).wait()
        local(shared_ref, shared_out, 3 + chunks).wait()
        own_factors.wait_send()
        shared_copy.wait_send()
        next_copy.wait_send()
        next_factors.wait_send()

    @pl.when(at.crosses)
    def _():
        own_factors.wait_recv()
        shared_copy.wait_recv()
        remote(factors_out.at[1 - at.tp], factors_out.at[1 - at.tp], factor_sems.at[2], at.next_core).wait_recv()

    offset_copy.wait_send()
    offset_came.wait_recv()
    local(offsets_ref, offsets_out.at[at.tp], 1 + chunks).wait()
    loads = [
        pltpu.make_async_copy(factors_out, factors_vm, out_sems.at[0]),
        pltpu.make_async_copy(offsets_out, offsets_vm, out_sems.at[1]),
        pltpu.make_async_copy(shared_out.at[:, pl.ds(0, width)], jd_vm, out_sems.at[2]),
    ]
    for load in loads:
        load.start()
    for load in loads:
        load.wait()

    kept = []

    def x_ready(i):
        span = pl.ds(i * ROWS, ROWS)

        @pl.when(at.crosses)
        def _():
            x_chunk(i).wait()

        @pl.when(holds)
        def _():
            local(tokens_ref.at[at.tp, span], x_vm.at[span], 1 + i).wait()

        keep = pltpu.make_async_copy(x_vm.at[span], x_out.at[span], x_sems.at[i, 2])
        keep.start()
        kept.append(keep)
        scaled, _ = row_norm(x_vm[span, :].astype(F32))
        xn = (scaled * gain_ref[...] + shift_ref[...]).astype(B16)
        xn_out[span, :] = xn
        u_out[span, :] = dot(xn, jd_vm[...], 1, 1).astype(B16)

    outs = (q_out, k_out, v_out)
    sending = []
    orders = ((0, 1, 2, 3), (1, 0, 2, 3), (2, 3, 1, 0), (3, 2, 1, 0))

    def plane_at(turn):
        plane = jnp.int32(orders[0][turn])
        for z in range(1, planes):
            plane = jnp.where(at.z == z, orders[z][turn], plane)
        return plane

    def to_next(turn):
        for flow in parts:
            flow.came(TP_CAME, plane_at(turn)).wait_recv()
            flow.copy(NEXT_SENT, plane_at(turn)).start()

    def w_load(turn):
        shards_of = pl.ds(2 * plane_at(turn), 2)
        return pltpu.make_async_copy(w_out.at[shards_of], w_vm.at[turn], out_sems.at[turn])

    def take_plane(turn):
        for flow in parts:
            flow.came(OWN_CAME, plane_at(turn)).wait_recv()
            flow.came(NEXT_CAME, plane_at(turn)).wait_recv()
        w_load(turn).start()

    def columns_of(turn):
        return pl.ds(pl.multiple_of(plane_at(turn) * 2 * depth, 2 * depth), 2 * depth)

    wide = rows_all // 2

    def product(turns, owner, part, span):
        value = 0.0
        for turn in turns:
            w = w_vm[turn, :, owner, part].reshape(2 * depth, half)
            value += dot(xn_out[span, columns_of(turn)], w)
        return value

    owners = (1 - at.core, at.core)

    def add_first(turns):
        for order, owner in enumerate(owners):
            for part in range(3):
                for begin in range(0, rows_all, wide):
                    span = pl.ds(begin, wide)
                    acc[order, part, span, :] = product(turns, owner, part, span)

    def add_last(turn):
        for order, owner in enumerate(owners):
            for part in range(3):
                bias = offsets_vm[owner, :, part * half : (part + 1) * half]
                up = factors_vm[owner, :, part * half : (part + 1) * half]
                for begin in range(0, rows_all, wide):
                    span = pl.ds(begin, wide)
                    value = acc[order, part, span, :] + bias + product((turn,), owner, part, span)
                    value += dot(u_out[span, :], up)
                    if part == 2:
                        stage[order, part, span, :] = value.astype(B16)
                        continue
                    for col in range(0, half, 128):
                        piece = value[:, col : col + 128]
                        stage[order, part, span, col : col + 128] = (
                            piece * cos_out[span, :] + partner(piece) * sin_out[span, :]
                        ).astype(B16)
                if order == 0:
                    move = remote(
                        stage.at[order, part], outs[part].at[pl.ds(rows_all, rows_all)],
                        move_sems.at[part], at.next_core,
                    )
                else:
                    move = pltpu.make_async_copy(
                        stage.at[order, part], outs[part].at[pl.ds(0, rows_all)], out_sems.at[4 + part]
                    )
                move.start()
                sending.append(move)

    to_next(0)
    to_next(1)
    for i in range(chunks):
        x_ready(i)
    for flow in parts:
        flow.pass_on(3, tp=True, core=True, wait=True)
    for other in ahead:
        other.pass_on(0, z=True)
    local(w_ref, w_out.at[at.shard, at.tp], 4 + chunks).wait()
    take_plane(0)
    take_plane(1)
    to_next(2)
    take_plane(2)
    for turn in range(3):
        w_load(turn).wait()
    add_first((0, 1, 2))
    to_next(3)
    take_plane(3)
    w_load(3).wait()
    add_last(3)

    for keep in kept:
        keep.wait()
    for other in ahead:
        other.wait(Z_CAME, 1)
        other.sent(0, z=True)
    for flow in parts:
        for far in range(planes):
            flow.sent(far, z=far < planes - 1, tp=True, core=True)
            flow.sent_next(far)
    for i in range(3):
        local((own_o, own_e, own_r)[i], (full_o, full_e, full_r)[i].at[at.shard, at.tp], 5 + i + chunks).wait()

    @pl.when(at.crosses)
    def _():
        spot_copy.wait_send()

    for move in sending:
        move.wait()


def project(planes, tokens, picks, places, bias, wide, tables, weight, own_o, own_e, own_r, gain, shift, rates):
    rows, width = tokens.shape[1:]
    _, depth, half = weight.shape
    rank = tables[0].shape[1]
    blocks = own_e.shape[1] // HIDDEN_BLOCK
    chunks = rows // ROWS
    shape = jax.ShapeDtypeStruct
    hbm = pl.BlockSpec(memory_space=pl.ANY)
    vmem = pl.BlockSpec(memory_space=pltpu.VMEM)
    smem = pl.BlockSpec(memory_space=pltpu.SMEM)
    dma = pltpu.SemaphoreType.DMA
    factors = shape((rank, 3 * half + sum(table.shape[2] for table in tables[5:])), B16)
    shared = shape((rank, 4 * width + 128), B16)
    offsets = shape((1, 3 * half + wide.shape[1]), F32)
    spots = shape(rates.shape[:1] + (rows,), B16)
    return pl.pallas_call(
        functools.partial(project_body, planes, blocks),
        in_specs=[hbm, smem] + [vmem] * 3 + [hbm] * 8 + [vmem] * 7,
        out_specs=[hbm] * 11 + [vmem] * 4,
        out_shape=[
            shape((rows, width), B16),
            shape((2,) + factors.shape, B16),
            shape(shared.shape, B16),
            shape((2,) + offsets.shape, F32),
            shape((2 * planes, 2) + weight.shape, B16),
            shape((2 * planes, 2) + own_o.shape, B16),
            shape((2 * planes, 2) + own_e.shape, B16),
            shape((2 * planes, 2) + own_r.shape, B16),
            shape((2 * rows, half), B16),
            shape((2 * rows, half), B16),
            shape((2 * rows, half), B16),
            shape((rows, width), B16),
            shape((rows, rank), B16),
            shape((2 * rows, 128), F32),
            shape((2 * rows, 128), F32),
        ],
        scratch_shapes=[
            pltpu.VMEM(spots.shape, B16),
            pltpu.VMEM(offsets.shape, F32),
            pltpu.VMEM(factors.shape, B16),
            pltpu.VMEM(factors.shape, B16),
            pltpu.VMEM(shared.shape, B16),
        ]
        + [pltpu.VMEM(table.shape, B16) for table in tables]
        + [
            pltpu.VMEM((rows, width), B16),
            pltpu.VMEM((planes, 2, 2) + weight.shape, B16),
            pltpu.VMEM((2, 3, rows, half), F32),
            pltpu.VMEM((2, 3, rows, half), B16),
            pltpu.VMEM((2,) + spots.shape, B16),
            pltpu.VMEM((2,) + factors.shape, B16),
            pltpu.VMEM((2,) + offsets.shape, F32),
            pltpu.VMEM((rank, width), B16),
            dma((3, 9, planes)),
            dma((count_rows(ALONG_Z, PROJECT_KINDS), planes)),
            dma((chunks, 3)),
            dma((2, 2)),
            dma((3, 2)),
            dma((2,)),
            dma((2,)),
            dma((8 + chunks,)),
            dma((7,)),
            dma((3, 2)),
            dma((8,)),
        ],
        compiler_params=pltpu.CompilerParams(
            vmem_limit_bytes=VMEM_LIMIT, collective_id=0, has_side_effects=True
        ),
        cost_estimate=pl.CostEstimate(
            flops=2 * rows * width * 6 * half, bytes_accessed=100 * 2**20, transcendentals=0
        ),
    )(tokens, picks, places, bias, wide, *tables, weight, own_o, own_e, own_r, gain, shift, rates)


def attend_body(
    planes, blocks,
    q_ref, k_ref, v_ref, cot_ref, own_o, own_e, own_r, in_o, in_e, in_r,
    o_ref, inv_ref, e_ref, o_next, cot_out, full_o, full_e, full_r,
    vm_ref, stage, cot_vm, flow_sems, stage_sems, cot_sems,
):
    at = Place(planes)
    rows_all, length = q_ref.shape[0], k_ref.shape[0]
    low = low_lanes()
    pair, turn = pl.program_id(0), pl.program_id(1)
    turns = length // rows_all
    now = pair * turns + turn
    pairs = stage.shape[0] // (turns // 2)
    count = pairs * turns
    taken = Rows(flow_sems)
    flow_o = Flow(at, own_o, lambda s, h: full_o.at[s, h], taken.take(EVERY), EVERY)
    flows = block_flows(at, own_e, own_r, full_e, full_r, taken, ATTEND_KINDS)
    zero = [flow_o] + flows[0]
    last = planes - 1
    cot_move = turned_copy(at, cot_ref.at[at.tp], cot_out, cot_sems)
    cot_load = pltpu.make_async_copy(cot_ref.at[at.tp], cot_vm, cot_sems.at[2])
    cot_keep = pltpu.make_async_copy(cot_vm, cot_out, cot_sems.at[3])

    def when(step, act):
        pl.when(now == min(step * count // 16, count - 1))(act)

    @pl.when(now == 0)
    def _():
        at.greet(True, True)
        for flow in zero:
            flow.pass_on(1, z=True)
            flow.pass_on(0, tp=True)
        pl.when(at.crosses)(lambda: cot_move.start())
        pl.when(jnp.logical_not(at.crosses))(lambda: cot_load.start())
        for flow in zero:
            flow.pass_on(0, core=True)
            flow.pass_on(1, core=True)
        for flow in flows[1] + flows[2]:
            flow.pass_on(0, core=True)

    def at_2():
        for flow in flows[1]:
            flow.pass_on(1, z=True, core=True)
        for flow in zero:
            flow.pass_on(1, tp=True)

    def at_3():
        @pl.when(jnp.logical_not(at.crosses))
        def _():
            cot_load.wait()
            cot_keep.start()

    def at_4():
        for flow in zero:
            flow.pass_on(2, z=True, tp=True, core=True, wait=True)

    def at_5():
        for flow in zero:
            flow.pass_next(0)

    def at_6():
        for flow in flows[1]:
            flow.pass_on(2, z=True, core=True, wait=True)
        for flow in flows[2]:
            flow.pass_on(0, z=True)

    def at_8():
        for flow in zero:
            flow.pass_on(3, tp=True, core=True, wait=True)

    def at_9():
        for flow in zero:
            flow.pass_next(1)
        for flow in flows[1]:
            flow.pass_on(0, tp=True)
            flow.pass_on(1, tp=True)

    def at_10():
        for flow in flows[2]:
            flow.pass_on(1, z=True, core=True, wait=True)
        for flow in flows[1]:
            flow.pass_on(3, core=True, wait=True)

    def at_12():
        for flow in flows[2]:
            flow.pass_on(2, z=True, core=True, wait=True)
        for flow in flows[3]:
            flow.pass_on(0, z=True)
        for flow in zero:
            flow.pass_next(2)
            flow.pass_next(3)

    def at_15():
        for flow in flows[2]:
            flow.pass_on(3, core=True, wait=True)

    for step, act in (
        (2, at_2), (3, at_3), (4, at_4), (5, at_5), (6, at_6), (8, at_8), (9, at_9), (10, at_10),
        (12, at_12), (15, at_15),
    ):
        when(step, act)

    @pl.when(turn == 0)
    def _():
        vm_ref[0] = jnp.where(low, v_ref[...], 1).astype(B16)
        vm_ref[1] = jnp.where(low, 1, v_ref[...]).astype(B16)

    step = min(256, rows_all)
    for begin in range(0, rows_all, step):
        rows = pl.ds(begin, step)
        q = q_ref[rows, :]
        sums = []
        for head in range(2):
            mine = low if head == 0 else ~low
            scores = dot(jnp.where(mine, q, 0).astype(B16), k_ref[...], 1, 1)
            top = jnp.max(scores, 1, keepdims=True)
            weights = jnp.exp2((scores - top) * exp_scale).astype(B16)
            e_ref[head, rows, :] = weights
            sums.append(dot(weights, vm_ref[head]))
        total = pltpu.roll(jnp.where(low, sums[1], sums[0]), 64, 1)
        inverse = 1.0 / total
        o_ref[rows, :] = (jnp.where(low, sums[0], sums[1]) * inverse).astype(B16)
        inv_ref[rows, :] = inverse

    def o_move(index):
        per = turns // 2
        rows = pl.ds(pl.multiple_of(index % per * rows_all, rows_all), rows_all)
        columns = pl.ds(pl.multiple_of(index // per * 128, 128), 128)
        return pltpu.make_async_remote_copy(
            src_ref=stage.at[index], dst_ref=o_next.at[rows, columns],
            send_sem=stage_sems.at[0, index], recv_sem=stage_sems.at[1, index],
            device_id=at.next_core, device_id_type=MESH,
        )

    @pl.when(turn >= turns // 2)
    def _():
        index = pair * (turns // 2) + turn - turns // 2
        stage[index] = o_ref[...]
        o_move(index).start()

    @pl.when(now == count - 1)
    def _():
        for flow in flows[3]:
            flow.wait(Z_CAME, 1)
        for flow in zero + flows[1] + flows[2]:
            for far in range(planes):
                flow.wait(OWN_CAME, far)
        for flow in zero:
            for far in range(planes):
                flow.wait(NEXT_CAME, far)
                flow.sent_next(far)
        for flow in flows[1]:
            for far in range(2):
                flow.wait(TP_CAME, far)
        for flow in zero + flows[1]:
            for far in range(planes):
                flow.sent(far, z=0 < far < last, tp=flow in zero or far < 2, core=True)
        for flow in flows[2]:
            for far in range(planes):
                flow.sent(far, z=far < last, core=True)
        for flow in flows[3]:
            flow.sent(0, z=True)

        @pl.when(at.crosses)
        def _():
            cot_move.wait()

        @pl.when(jnp.logical_not(at.crosses))
        def _():
            cot_keep.wait()

        for index in range(count // 2):
            o_move(index).wait()


def attend(planes, query, key, value, cotangent, own_o, own_e, own_r, full_o, full_e, full_r):
    length, width = query.shape
    block = min(512, length // 2)
    blocks = own_e.shape[1] // HIDDEN_BLOCK
    turns = length // block
    pairs = width // 128
    rows = pl.BlockSpec((block, 128), lambda p, i: (i, p))
    full = pl.BlockSpec((length, 128), lambda p, i: (0, p))
    hbm = pl.BlockSpec(memory_space=pl.ANY)
    shape = jax.ShapeDtypeStruct
    like = lambda array: shape(array.shape, array.dtype)
    dma = pltpu.SemaphoreType.DMA
    return pl.pallas_call(
        functools.partial(attend_body, planes, blocks),
        grid=(pairs, turns),
        in_specs=[rows, full, full] + [hbm] * 7,
        out_specs=[rows, rows, pl.BlockSpec((2, block, length), lambda p, i: (p, i, 0))] + [hbm] * 5,
        out_shape=[
            shape((length, width), B16),
            shape((length, width), F32),
            shape((width // 64, length, length), B16),
            shape((length // 2, width), B16),
            shape(cotangent.shape[1:], B16),
            like(full_o), like(full_e), like(full_r),
        ],
        input_output_aliases={7: 5, 8: 6, 9: 7},
        scratch_shapes=[
            pltpu.VMEM((2, length, 128), B16),
            pltpu.VMEM((pairs * turns // 2, block, 128), B16),
            pltpu.VMEM(cotangent.shape[1:], B16),
            dma((count_rows(EVERY, ATTEND_KINDS), planes)),
            dma((2, pairs * turns // 2)),
            dma((4,)),
        ],
        compiler_params=pltpu.CompilerParams(
            vmem_limit_bytes=VMEM_LIMIT, collective_id=1, has_side_effects=True
        ),
        cost_estimate=pl.CostEstimate(
            flops=16 * length * length * width,
            bytes_accessed=width // 64 * length * length * 2,
            transcendentals=width // 64 * length * length,
        ),
    )(query, key, value, cotangent, own_o, own_e, own_r, full_o, full_e, full_r)


def attend_back_body(
    planes,
    q_ref, k_ref, v_ref, o_ref, inv_ref, g_ref, e_ref, cos_ref, sin_ref, cos_all, sin_all,
    split_ref, full_ref, tag_ref, out_ref,
    own_ref, other_ref, sums_ref, home_ref,
    key_sum, value_sum, vm_ref, q_stage, kv_stage, out_vm, move_sems, out_sems, *spread_refs,
):
    at = Place(planes)
    rows_all, length = q_ref.shape[0], k_ref.shape[0]
    low = low_lanes()
    pair, at_step = pl.program_id(0), pl.program_id(1)
    pairs, turns = q_stage.shape[0], q_stage.shape[1]
    now = pair * turns + at_step
    count = pairs * turns
    local_rows = length // 2
    spread = Spread(at, split_ref, full_ref, tag_ref[...], sums_ref, *spread_refs)
    stays = jnp.logical_not(at.crosses)
    out_load = pltpu.make_async_copy(out_ref, out_vm, out_sems.at[0])
    out_keep = pltpu.make_async_copy(out_vm, home_ref.at[at.tp], out_sems.at[1])
    out_turn = pltpu.make_async_remote_copy(
        src_ref=out_ref, dst_ref=home_ref.at[at.tp], send_sem=out_sems.at[2], recv_sem=out_sems.at[3],
        device_id=at.turned, device_id_type=MESH,
    )

    def out_tp(source):
        return pltpu.make_async_remote_copy(
            src_ref=source, dst_ref=home_ref.at[at.tp], send_sem=out_sems.at[4], recv_sem=out_sems.at[5],
            device_id=at.next_tp, device_id_type=MESH,
        )

    def when(step, act):
        pl.when(now == step)(act)

    @pl.when(now == 0)
    def _():
        pl.when(stays)(lambda: out_load.start())
        at.greet(True, True, True)
        spread.start()
        pl.when(at.crosses)(lambda: out_turn.start())

    when(2, spread.second)

    @pl.when(now == 3)
    def _():
        @pl.when(stays)
        def _():
            out_load.wait()
            out_keep.start()
            out_tp(out_vm).start()

    when(4, spread.third)
    when(6, lambda: spread.planes(0))

    @pl.when(now == 7)
    def _():
        @pl.when(at.crosses)
        def _():
            out_turn.wait_recv()
            out_tp(home_ref.at[at.tp]).start()

    when(9, lambda: spread.planes(1))
    when(12, lambda: spread.planes(2))
    when(15, lambda: spread.planes(3))

    @pl.when(at_step == 0)
    def _():
        key_sum[...] = jnp.zeros_like(key_sum)
        value_sum[...] = jnp.zeros_like(value_sum)
        vm_ref[0] = jnp.where(low, v_ref[...], -1).astype(B16)
        vm_ref[1] = jnp.where(low, -1, v_ref[...]).astype(B16)

    step = min(256, rows_all)
    for begin in range(0, rows_all, step):
        rows = pl.ds(begin, step)
        grad = g_ref[rows, :].astype(F32) * inv_ref[rows, :]
        grad_low = grad.astype(B16)
        product = pltpu.roll(grad * o_ref[rows, :].astype(F32), 64, 1).astype(B16)
        q_turned = q_ref[rows, :].T
        g_turned = grad_low.T
        parts = []
        for head in range(2):
            mine = low if head == 0 else ~low
            weights = e_ref[head, rows, :]
            grad_probs = dot(jnp.where(mine, grad_low, product), vm_ref[head], 1, 1)
            grad_scores = (weights.astype(F32) * grad_probs).astype(B16)
            parts.append(dot(grad_scores, k_ref[...]))
            span = pl.ds(head * 64, 64)
            key_sum[span, :] += dot(q_turned[head * 64 : head * 64 + 64], grad_scores)
            value_sum[span, :] += dot(g_turned[head * 64 : head * 64 + 64], weights)
        gq = jnp.where(low, parts[0], parts[1]) * score_scale
        q_stage[pair, at_step, rows, :] = (
            gq * cos_ref[rows, :] + partner(gq * sin_ref[rows, :])
        ).astype(B16)

    def columns(index):
        return pl.ds(pl.multiple_of(index * 128, 128), 128)

    def q_here(pair_index, turn_index):
        rows = pl.ds(pl.multiple_of(turn_index * rows_all, rows_all), rows_all)
        return pltpu.make_async_copy(
            q_stage.at[pair_index, turn_index], own_ref.at[0, rows, columns(pair_index)],
            move_sems.at[0, pair_index * turns + turn_index],
        )

    def q_there(pair_index, turn_index):
        rows = pl.ds(pl.multiple_of(turn_index * rows_all - local_rows, rows_all), rows_all)
        index = pair_index * turns + turn_index
        return pltpu.make_async_remote_copy(
            src_ref=q_stage.at[pair_index, turn_index], dst_ref=other_ref.at[0, rows, columns(pair_index)],
            send_sem=move_sems.at[0, index], recv_sem=move_sems.at[1, index],
            device_id=at.next_core, device_id_type=MESH,
        )

    def kv_here(part, pair_index):
        return pltpu.make_async_copy(
            kv_stage.at[part, pair_index, pl.ds(0, local_rows)], own_ref.at[1 + part, :, columns(pair_index)],
            move_sems.at[2, 2 * pair_index + part],
        )

    def kv_there(part, pair_index):
        index = 2 * pair_index + part
        return pltpu.make_async_remote_copy(
            src_ref=kv_stage.at[part, pair_index, pl.ds(local_rows, local_rows)],
            dst_ref=other_ref.at[1 + part, :, columns(pair_index)],
            send_sem=move_sems.at[3, index], recv_sem=move_sems.at[4, index],
            device_id=at.next_core, device_id_type=MESH,
        )

    pl.when(at_step < turns // 2)(lambda: q_here(pair, at_step).start())
    pl.when(at_step >= turns // 2)(lambda: q_there(pair, at_step).start())

    @pl.when(at_step == turns - 1)
    def _():
        gk = key_sum[...].T * score_scale
        kv_stage[0, pair] = (gk * cos_all[...] + partner(gk * sin_all[...])).astype(B16)
        kv_stage[1, pair] = value_sum[...].T.astype(B16)
        for part in range(2):
            kv_here(part, pair).start()
            kv_there(part, pair).start()

    @pl.when(now == count - 1)
    def _():
        for pair_index in range(pairs):
            for turn_index in range(turns):
                if turn_index < turns // 2:
                    q_here(pair_index, turn_index).wait()
                else:
                    q_there(pair_index, turn_index).wait()
            for part in range(2):
                kv_here(part, pair_index).wait()
                kv_there(part, pair_index).wait()
        spread.finish()
        spread.sent()

        @pl.when(stays)
        def _():
            out_keep.wait()
            out_tp(out_vm).wait_send()

        @pl.when(at.crosses)
        def _():
            out_turn.wait_send()
            out_tp(home_ref.at[at.tp]).wait_send()

        pltpu.make_async_remote_copy(
            src_ref=home_ref.at[at.tp], dst_ref=home_ref.at[1 - at.tp], send_sem=out_sems.at[4],
            recv_sem=out_sems.at[5], device_id=at.next_tp, device_id_type=MESH,
        ).wait_recv()


def attend_back(planes, query, key, value, attended, inverse, grad, weights, cosine, sine, split, full, tag, out, adapters):
    length, width = query.shape
    block = min(512, length // 2)
    pairs, turns = width // 128, length // block
    rows = pl.BlockSpec((block, 128), lambda p, i: (i, p))
    whole = pl.BlockSpec((length, 128), lambda p, i: (0, p))
    table = pl.BlockSpec((block, 128), lambda p, i: (i, 0))
    one = lambda array: pl.BlockSpec(
        array.shape, lambda p, i: (0,) * len(array.shape), pipeline_mode=pl.Buffered(1)
    )
    hbm = pl.BlockSpec(memory_space=pl.ANY)
    shape = jax.ShapeDtypeStruct
    dma = pltpu.SemaphoreType.DMA
    ranks = full.shape[0] // 2
    keep = split.shape[2] + full.shape[1]
    sums = shape((adapters, 2 * ranks, keep), F32)
    return pl.pallas_call(
        functools.partial(attend_back_body, planes),
        grid=(pairs, turns),
        in_specs=[
            rows, whole, whole, rows, rows, rows,
            pl.BlockSpec((2, block, length), lambda p, i: (p, i, 0)),
            table, table, one(cosine), one(sine), one(split), one(full), one(tag), hbm,
        ],
        out_specs=[hbm, hbm, one(sums), hbm],
        out_shape=[
            shape((3, length // 2, width), B16), shape((3, length // 2, width), B16), sums,
            shape((2,) + out.shape, B16),
        ],
        scratch_shapes=[
            pltpu.VMEM((128, length), F32),
            pltpu.VMEM((128, length), F32),
            pltpu.VMEM((2, length, 128), B16),
            pltpu.VMEM((pairs, turns, block, 128), B16),
            pltpu.VMEM((2, pairs, length, 128), B16),
            pltpu.VMEM(out.shape, B16),
            dma((5, max(pairs * turns, 2 * pairs))),
            dma((6,)),
        ]
        + Spread.scratch(planes, ranks, split.shape[2], full.shape[1]),
        compiler_params=pltpu.CompilerParams(
            vmem_limit_bytes=VMEM_LIMIT, collective_id=3, has_side_effects=True
        ),
        cost_estimate=pl.CostEstimate(
            flops=20 * length * length * width,
            bytes_accessed=width // 64 * length * length * 2,
            transcendentals=0,
        ),
    )(query, key, value, attended, inverse, grad, weights, cosine, sine, cosine, sine, split, full, tag, out)


def gauss_parts(z):
    t = 1.0 / (1.0 + (0.3275911 * math.sqrt(0.5)) * jnp.abs(z))
    poly = t * (0.254829592 + t * (-0.284496736 + t * (1.421413741 + t * (-1.453152027 + t * 1.061405429))))
    bell = jnp.exp2((z * z) * (-0.5 * math.log2(math.e)))
    upper = 0.5 * poly * bell
    cdf = jnp.where(z >= 0, 1.0 - upper, upper)
    return cdf, bell * (1.0 / math.sqrt(2.0 * math.pi))


def middle_body(
    planes, blocks,
    x_ref, cot_ref, own_ref, other_ref, wo_ref, factors_ref, shared_ref, offsets_ref,
    out_off, gain_ref, shift_ref, shrink_off, in_e, in_r,
    output_ref, gh_ref, t_split, t_full, gatt_out, full_e, full_r,
    hidden, xn_ref, total, back, u2_ref, u3_ref, u4_sum, g4_ref, g3_sum,
    e_vm, r_vm, gown_vm, gother_vm, load_sems, flow_sems, grad_sems,
):
    at = Place(planes)
    f = pl.program_id(0)
    last = 2 * blocks - 1
    core = at.core
    rows_all, width = x_ref.shape
    half = own_ref.shape[1]
    hidden_half = blocks * HIDDEN_BLOCK
    step = 256
    flows = block_flows(at, None, None, full_e, full_r, Rows(flow_sems), MIDDLE_KINDS)
    planes_all = range(planes)

    def pass_on(pair, **how):
        for flow in pair:
            for far in planes_all:
                flow.pass_on(far, fresh=False, **how)

    def pass_next(pair, wait):
        for flow in pair:
            for far in planes_all:
                flow.pass_next(far, wait)

    def arrived(pair, kind):
        for flow in pair:
            for far in planes_all:
                flow.wait(kind, far)

    def loads(index, slot):
        tp_half = jnp.where(index < blocks, at.tp, 1 - at.tp)
        span = pl.ds(pl.multiple_of(index % blocks * HIDDEN_BLOCK, HIDDEN_BLOCK), HIDDEN_BLOCK)
        return (
            pltpu.make_async_copy(full_e.at[:, tp_half, :, span], e_vm.at[slot], load_sems.at[0, slot]),
            pltpu.make_async_copy(full_r.at[:, tp_half, span, :], r_vm.at[slot], load_sems.at[1, slot]),
        )

    def wo_half(part):
        w = wo_ref[:, part]
        return jnp.concatenate([w[i] for i in range(w.shape[0])], axis=1)

    jd, ed, ou, ru = (pl.ds(i * width, width) for i in range(4))
    od = pl.ds(3 * half, half)

    @pl.when(f == 0)
    def _():
        for load in loads(0, 0):
            load.start()
        at.greet(True, False)
        for flow in flows[3]:
            flow.pass_on(1, fresh=False, z=True, core=True)
            flow.pass_on(0, fresh=False, core=True)
        for flow in flows[1]:
            flow.pass_on(2, fresh=False, tp=True)
            flow.pass_on(3, fresh=False, tp=True)
            flow.pass_next(0, False)
            flow.pass_next(1, False)
        pass_on(flows[2], tp=True)
        w_own, w_other = wo_half(core), wo_half(1 - core)
        for begin in range(0, rows_all, step):
            rows = pl.ds(begin, step)
            own, other = own_ref[rows, :], other_ref[rows, :]
            u2 = (
                dot(own, factors_ref[core, :, od], 1, 1) + dot(other, factors_ref[1 - core, :, od], 1, 1)
            ).astype(B16)
            u2_ref[rows, :] = u2
            h = (
                x_ref[rows, :].astype(F32) + dot(own, w_own) + dot(other, w_other)
                + out_off[...] + dot(u2, shared_ref[:, ou])
            )
            hidden[rows, :] = h
            scaled, _ = row_norm(h)
            xn = (scaled * gain_ref[...] + shift_ref[...]).astype(B16)
            xn_ref[rows, :] = xn
            u3_ref[rows, :] = dot(xn, shared_ref[:, ed], 1, 1).astype(B16)
            g4_ref[rows, :] = dot(cot_ref[rows, :], shared_ref[:, ru], 1, 1).astype(B16)
            total[rows, :] = h + shrink_off[...]
            back[rows, :] = jnp.zeros_like(h)
            u4_sum[rows, :] = jnp.zeros((step, u4_sum.shape[1]), F32)
            g3_sum[rows, :] = jnp.zeros((step, g3_sum.shape[1]), F32)
        for flow in flows[3]:
            flow.pass_on(2, fresh=False, z=True, core=True, wait=True)

    @pl.when(f == 1)
    def _():
        for flow in flows[3]:
            flow.pass_on(3, fresh=False, core=True, wait=True)

    @pl.when(f == 2)
    def _():
        pass_on(flows[3], tp=True)
        arrived(flows[3], OWN_CAME)

    @pl.when(f == 3)
    def _():
        for flow in flows[1]:
            flow.pass_next(2)
            flow.pass_next(3)

    @pl.when(f == 4)
    def _():
        arrived(flows[1], NEXT_CAME)

    @pl.when(f == last - 2)
    def _():
        pass_next(flows[2], True)

    slot = f % 2

    @pl.when(f < last - 2)
    def _():
        for load in loads(f + 1, 1 - slot):
            load.start()

    for load in loads(f, slot):
        load.wait()
    tp_half = jnp.where(f < blocks, at.tp, 1 - at.tp)
    begin_block = f % blocks * HIDDEN_BLOCK

    def block_of(first):
        return pl.ds(pl.multiple_of(first + begin_block, 128), HIDDEN_BLOCK)

    w_e = e_vm[slot].reshape(width, HIDDEN_BLOCK)
    w_r = jnp.concatenate([r_vm[slot, i] for i in range(2 * planes)], axis=1)
    eu = factors_ref[tp_half, :, block_of(4 * half)]
    rd = factors_ref[tp_half, :, block_of(4 * half + hidden_half)]
    wide_off = offsets_ref[tp_half, :, block_of(3 * half)]
    u3, g4 = u3_ref[...], g4_ref[...]
    z = dot(xn_ref[...], w_e) + wide_off + dot(u3, eu)
    gact = dot(cot_ref[...], w_r, 1, 1) + dot(g4, rd)
    cdf, density = gauss_parts(z)
    act = (z * cdf).astype(B16)
    gz = (gact * (cdf + z * density)).astype(B16)
    total[...] += dot(act, w_r)
    u4_sum[...] += dot(act, rd, 1, 1)
    back[...] += dot(gz, w_e, 1, 1)
    g3_sum[...] += dot(gz, eu, 1, 1)
    sum_rd = dot(g4, act, 0, 0)
    sum_eu = dot(u3, gz, 0, 0)
    t_split[tp_half, :, block_of(half + hidden_half)] = sum_rd
    t_split[tp_half, :, block_of(half)] = sum_eu

    @pl.when(f == last - 2)
    def _():
        arrived(flows[2], NEXT_CAME)

    @pl.when(f == last - 1)
    def _():
        pass_next(flows[3], True)
        arrived(flows[3], NEXT_CAME)

    @pl.when((f == last - 2) | (f == last - 1))
    def _():
        for load in loads(f + 1, 1 - slot):
            load.start()

    @pl.when(f == last)
    def _():
        w_own, w_other = wo_half(core), wo_half(1 - core)
        s_ru, s_ed, s_ou, s_own, s_other = 0.0, 0.0, 0.0, 0.0, 0.0
        moves = []
        for index, begin in enumerate(range(0, rows_all, step)):
            rows = pl.ds(begin, step)
            cot = cot_ref[rows, :]
            u4 = u4_sum[rows, :].astype(B16)
            output_ref[rows, :] = (total[rows, :] + dot(u4, shared_ref[:, ru])).astype(B16)
            s_ru += dot(u4, cot, 0, 0)
            g3 = g3_sum[rows, :].astype(B16)
            s_ed += dot(g3, xn_ref[rows, :], 0, 0)
            gx = back[rows, :] + dot(g3, shared_ref[:, ed])
            scaled, inverse = row_norm(hidden[rows, :])
            gh = cot.astype(F32) + back_norm(gx * gain_ref[...], scaled, inverse)
            gh_ref[rows, :] = gh
            gb = gh.astype(B16)
            s_ou += dot(u2_ref[rows, :], gb, 0, 0)
            g2 = dot(gb, shared_ref[:, ou], 1, 1).astype(B16)
            s_own += dot(g2, own_ref[rows, :], 0, 0)
            s_other += dot(g2, other_ref[rows, :], 0, 0)
            gother_vm[rows, :] = (
                dot(gb, w_other, 1, 1) + dot(g2, factors_ref[1 - core, :, od])
            ).astype(B16)
            there = pltpu.make_async_remote_copy(
                src_ref=gother_vm.at[rows], dst_ref=gatt_out.at[pl.ds(rows_all + begin, step)],
                send_sem=grad_sems.at[0, index], recv_sem=grad_sems.at[1, index],
                device_id=at.next_core, device_id_type=MESH,
            )
            there.start()
            gown_vm[rows, :] = (dot(gb, w_own, 1, 1) + dot(g2, factors_ref[core, :, od])).astype(B16)
            here = pltpu.make_async_copy(gown_vm.at[rows], gatt_out.at[rows], grad_sems.at[2, index])
            here.start()
            moves += [there, here]
        t_full[:, 0:width] = s_ou
        t_full[:, width : 2 * width] = s_ed
        t_full[:, 2 * width :] = s_ru
        t_split[core, :, 0:half] = s_own
        t_split[1 - core, :, 0:half] = s_other
        for index, pair in enumerate(flows[1:]):
            for flow in pair:
                for far in planes_all:
                    flow.sent(far, z=index == 2 and far in (1, 2), tp=index > 0 or far > 1, core=index == 2)
                    flow.sent_next(far)
        for move in moves:
            move.wait()


def middle(
    planes, x, cot, attended, other, w_o, factors, shared, offsets, out_off, gain, shift, shrink_off, w_e, w_r
):
    rows, width = x.shape
    half = attended.shape[1]
    shards_, _, depth, hidden_half = w_e.shape
    rank = factors.shape[1]
    blocks = hidden_half // HIDDEN_BLOCK
    one = lambda shape: pl.BlockSpec(
        shape, lambda f: (0,) * len(shape), pipeline_mode=pl.Buffered(1)
    )
    hbm = pl.BlockSpec(memory_space=pl.ANY)
    shape = jax.ShapeDtypeStruct
    dma = pltpu.SemaphoreType.DMA
    chunks = rows // 256
    return pl.pallas_call(
        functools.partial(middle_body, planes, blocks),
        grid=(2 * blocks,),
        in_specs=[
            one((rows, width)), one((rows, width)), one((rows, half)), one((rows, half)),
            one(w_o.shape), one(factors.shape), one(shared.shape), one(offsets.shape),
            one((1, width)), one((1, width)), one((1, width)), one((1, width)), hbm, hbm,
        ],
        out_specs=[
            one((rows, width)), one((rows, width)),
            one((2, rank, half + 2 * hidden_half)), one((rank, 3 * width)), hbm, hbm, hbm,
        ],
        out_shape=[
            shape((rows, width), B16), shape((rows, width), F32),
            shape((2, rank, half + 2 * hidden_half), F32), shape((rank, 3 * width), F32),
            shape((2 * rows, half), B16), shape(w_e.shape, B16), shape(w_r.shape, B16),
        ],
        input_output_aliases={12: 5, 13: 6},
        scratch_shapes=[
            pltpu.VMEM((rows, width), F32), pltpu.VMEM((rows, width), B16),
            pltpu.VMEM((rows, width), F32), pltpu.VMEM((rows, width), F32),
            pltpu.VMEM((rows, rank), B16), pltpu.VMEM((rows, rank), B16),
            pltpu.VMEM((rows, rank), F32), pltpu.VMEM((rows, rank), B16),
            pltpu.VMEM((rows, rank), F32),
            pltpu.VMEM((2, shards_, depth, HIDDEN_BLOCK), B16),
            pltpu.VMEM((2, shards_, HIDDEN_BLOCK, w_r.shape[3]), B16),
            pltpu.VMEM((rows, half), B16), pltpu.VMEM((rows, half), B16),
            dma((2, 2)), dma((count_rows((), MIDDLE_KINDS), planes)), dma((3, chunks)),
        ],
        compiler_params=pltpu.CompilerParams(
            vmem_limit_bytes=VMEM_LIMIT, collective_id=2, has_side_effects=True
        ),
        cost_estimate=pl.CostEstimate(
            flops=2 * rows * width * (16 * hidden_half // 2 + 4 * half),
            bytes_accessed=40 * 2**20,
            transcendentals=rows * hidden_half * 2,
        ),
    )(x, cot, attended, other, w_o, factors, shared, offsets, out_off, gain, shift, shrink_off, w_e, w_r)


def unproject_body(
    planes,
    x_ref, gh_ref, xn_ref, u_ref, gain_ref, w_ref, factors_ref, shared_ref, own_ref, other_ref,
    home_ref, sums_ref,
    own_vm, other_vm, w_vm, x_vm, gh_vm, xn_vm, stage, split, full, g1_vm, load_sems, move_sems, *spread_refs,
):
    at = Place(planes)
    rows_all, width = x_vm.shape
    half = own_vm.shape[2]
    core = at.core
    spread = Spread(at, split, full, shared_ref[0:8, 4 * width :], sums_ref, *spread_refs)
    halves = ((own_vm, core), (other_vm, 1 - core))
    chunks = rows_all // ROWS

    def load(index, source, target):
        return pltpu.make_async_copy(source, target, load_sems.at[index])

    loads = [load(0, own_ref, own_vm), load(1, other_ref, other_vm), load(2, xn_ref, xn_vm)]
    late = [load(3, x_ref, x_vm), load(4, gh_ref, gh_vm)]
    late += [load(5 + order, w_ref.at[:, owner], w_vm.at[order]) for order, (_, owner) in enumerate(halves)]
    for item in loads + late:
        item.start()
    at.greet(True, True, True, True)
    for item in loads:
        item.wait()
    u = u_ref[...]
    g1 = 0.0
    for source, owner in halves:
        for part in range(3):
            columns = pl.ds(part * half, half)
            g1 += dot(source[part], factors_ref[owner, :, columns], 1, 1)
            split[owner, :, columns] = dot(u, source[part], 0, 0)
    g1 = g1.astype(B16)
    g1_vm[...] = g1
    full[...] = dot(g1, xn_vm[...], 0, 0)
    spread.start()
    order = [2, 0, 3, 1]
    for item in late:
        item.wait()
    quarter = rows_all // 2

    def moves(i):
        tp_half = i * ROWS // quarter
        rows = pl.ds(i * ROWS % quarter, ROWS)
        source, target = stage.at[i], home_ref.at[at.tp, rows]

        def remote(device, came):
            return pltpu.make_async_remote_copy(
                src_ref=source, dst_ref=target, send_sem=move_sems.at[0, i], recv_sem=move_sems.at[came, i],
                device_id=device, device_id_type=MESH,
            )

        mine = at.tp == tp_half
        both = dict(at.turned)
        both["tp"] = 1 - at.tp
        return (
            (mine & jnp.logical_not(at.crosses), lambda: pltpu.make_async_copy(source, target, move_sems.at[0, i]), True),
            (mine & at.crosses, lambda: remote(at.turned, 1), False),
            (jnp.logical_not(mine) & jnp.logical_not(at.crosses), lambda: remote(at.next_tp, 2), False),
            (jnp.logical_not(mine) & at.crosses, lambda: remote(both, 2), False),
        )

    stages = [spread.second, spread.third, lambda: spread.planes(0), lambda: spread.planes(1)]
    for count, i in enumerate(order):
        span = pl.ds(i * ROWS, ROWS)
        gx = dot(g1_vm[span, :], shared_ref[:, 0:width])
        for index, (source, _) in enumerate(halves):
            for part in range(3):
                gx += dot(source[part, span, :], w_vm[index, :, part].reshape(width, half), 1, 1)
        scaled, inverse = row_norm(x_vm[span, :].astype(F32))
        stage[i] = (gh_vm[span, :] + back_norm(gx * gain_ref[...], scaled, inverse)).astype(B16)
        for there, move, _ in moves(i):
            pl.when(there)(lambda move=move: move().start())
        stages[count]()
    for distance in range(2, planes):
        spread.planes(distance)
    spread.finish()
    spread.sent()
    for i in range(chunks):
        for there, move, here in moves(i):
            if here:
                pl.when(there)(lambda move=move: move().wait())
            else:
                pl.when(there)(lambda move=move: move().wait_send())
    for i in range(chunks):
        tp_half = i * ROWS // quarter
        rows = pl.ds(i * ROWS % quarter, ROWS)

        def came(slot):
            return pltpu.make_async_remote_copy(
                src_ref=stage.at[i], dst_ref=home_ref.at[slot, rows], send_sem=move_sems.at[0, i],
                recv_sem=move_sems.at[1, i], device_id=at.next_tp, device_id_type=MESH,
            )

        pl.when((at.tp == tp_half) & at.crosses)(lambda came=came: came(at.tp).wait_recv())

    for i in range(chunks):
        tp_half = i * ROWS // quarter
        rows = pl.ds(i * ROWS % quarter, ROWS)

        def came(slot):
            return pltpu.make_async_remote_copy(
                src_ref=stage.at[i], dst_ref=home_ref.at[slot, rows], send_sem=move_sems.at[0, i],
                recv_sem=move_sems.at[2, i], device_id=at.next_tp, device_id_type=MESH,
            )

        pl.when(at.tp == tp_half)(lambda came=came: came(1 - at.tp).wait_recv())


def unproject(planes, x, gh, xn, u, gain, weight, factors, shared, own, other, adapters):
    rows, width = x.shape
    half = own.shape[2]
    rank = factors.shape[1]
    hbm = pl.BlockSpec(memory_space=pl.ANY)
    vmem = pl.BlockSpec(memory_space=pltpu.VMEM)
    shape = jax.ShapeDtypeStruct
    dma = pltpu.SemaphoreType.DMA
    chunks = rows // ROWS
    keep = 3 * half + width
    return pl.pallas_call(
        functools.partial(unproject_body, planes),
        in_specs=[hbm, hbm, hbm, vmem, vmem, hbm, vmem, vmem, hbm, hbm],
        out_specs=[hbm, vmem],
        out_shape=[shape((2, rows // 2, width), B16), shape((adapters, rank, keep), F32)],
        scratch_shapes=[
            pltpu.VMEM(own.shape, B16), pltpu.VMEM(own.shape, B16),
            pltpu.VMEM((2, weight.shape[0]) + weight.shape[2:], B16),
            pltpu.VMEM((rows, width), B16), pltpu.VMEM((rows, width), F32), pltpu.VMEM((rows, width), B16),
            pltpu.VMEM((chunks, ROWS, width), B16),
            pltpu.VMEM((2, rank, 3 * half), F32), pltpu.VMEM((rank, width), F32), pltpu.VMEM((rows, rank), B16),
            dma((7,)), dma((3, chunks)),
        ]
        + Spread.scratch(planes, rank // 2, 3 * half, width),
        compiler_params=pltpu.CompilerParams(
            vmem_limit_bytes=VMEM_LIMIT, collective_id=4, has_side_effects=True
        ),
        cost_estimate=pl.CostEstimate(
            flops=2 * rows * width * 6 * half, bytes_accessed=20 * 2**20, transcendentals=0
        ),
    )(x, gh, xn, u, gain, weight, factors, shared, own, other)


def rate_parts():
    lane = np.arange(128) % 64
    rates = np.exp((lane % 10).astype(np.float32) * np.float32(-math.log(10000.0) / 10.0)).astype(np.float32)
    rates = np.where(lane[None] // 20 == np.arange(3)[:, None], rates[None], np.float32(0.0)).astype(np.float32)
    parts = []
    for _ in range(3):
        part = rates.astype(ml_dtypes.bfloat16)
        parts.append(part)
        rates = rates - part.astype(np.float32)
    parts.append(np.zeros((7, 128), ml_dtypes.bfloat16))
    return jnp.asarray(np.concatenate(parts, axis=0))


def clip_shards(
    planes,
    tokens,
    cotangent,
    adapter_pick,
    positions,
    first_gain,
    first_shift,
    joined_weight,
    joined_bias,
    output_weight,
    mixing_exit_offset,
    second_gain,
    second_shift,
    expand_weight,
    widening_offset,
    reduce_weight,
    shrinking_offset,
    joined_down,
    joined_up,
    output_down,
    output_up,
    expand_down,
    expand_up,
    reduce_down,
    reduce_up,
):
    half = joined_weight.shape[2]
    hidden_half = expand_weight.shape[1]
    rank = joined_up.shape[1]
    turn_last = lambda array: jnp.swapaxes(array, 1, 2)
    tables = (
        turn_last(joined_down), turn_last(expand_down), output_up, reduce_up,
        turn_last(joined_up), turn_last(output_down), expand_up, turn_last(reduce_down),
    )
    (
        x, factors, shared, offsets, w_j, w_o, w_e, w_r, query, key, value, xn1, u1, cosine, sine,
    ) = project(
        planes, tokens, adapter_pick, positions, joined_bias, widening_offset[None], tables,
        jnp.transpose(joined_weight, (1, 0, 2)), output_weight, expand_weight, reduce_weight,
        first_gain[None], first_shift[None], rate_parts(),
    )
    attended, inverse, weights, other_heads, cot, w_o, w_e, w_r = attend(
        planes, query, key, value, cotangent, output_weight, expand_weight, reduce_weight, w_o, w_e, w_r
    )
    out, gh, split, full, grad_att, w_e, w_r = middle(
        planes, x, cot, attended, other_heads, w_o, factors, shared, offsets,
        mixing_exit_offset[None], second_gain[None], second_shift[None], shrinking_offset[None], w_e, w_r,
    )
    adapters = joined_down.shape[0]
    width = tokens.shape[2]
    tag = shared[: rank // 2, 4 * width :]
    own, other, sums, output = attend_back(
        planes, query, key, value, attended, inverse, grad_att, weights, cosine, sine, split, full, tag, out, adapters
    )
    tokens_grad, late_sums = unproject(
        planes, x, gh, xn1, u1, first_gain[None], w_j, factors, shared, own, other, adapters
    )

    def cut(array, *sizes):
        begin, pieces = 0, []
        for size in sizes:
            pieces.append(array[:, :, begin : begin + size])
            begin += size
        return pieces

    s_od, s_eu, s_rd, s_ou, s_ed, s_ru = cut(sums, half, hidden_half, hidden_half, width, width, width)
    s_fu, s_fd = cut(late_sums, 3 * half, width)
    return (
        output,
        tokens_grad,
        turn_last(s_fd),
        s_fu.reshape(adapters, rank, 3, half),
        turn_last(s_od),
        s_ou,
        turn_last(s_ed),
        s_eu,
        turn_last(s_rd),
        s_ru,
    )


def solution(mesh):
    sizes = dict(mesh.shape)
    if sizes["ctx"] == 2 and sizes["tp"] == 2 and sizes["shard"] == 8:
        body = functools.partial(clip_shards, sizes["shard"] // 2)
    else:
        body = general_shards
    return jax.shard_map(
        body,
        mesh=mesh,
        in_specs=(
            P("shard", "ctx", None),
            P("shard", "ctx", None),
            P("shard"),
            P(None, "shard", "ctx"),
            P(),
            P(),
            P("shard", None, "tp"),
            P(None, "tp"),
            P("tp", "shard"),
            P(),
            P(),
            P(),
            P("shard", "tp"),
            P("tp"),
            P("tp", "shard"),
            P(),
            P(),
            P(None, None, None, "tp"),
            P(None, "tp", None),
            P(),
            P(),
            P(None, None, "tp"),
            P(None, "tp", None),
            P(),
        ),
        out_specs=(
            P("shard", "ctx", None),
            P("shard", ("ctx", "tp"), None),
            P(),
            P(None, None, None, "tp"),
            P(None, "tp", None),
            P(),
            P(),
            P(None, None, "tp"),
            P(None, "tp", None),
            P(),
        ),
        check_vma=False,
    )
```

profile of v0, /device:TPU:0, one launch (start us, length us, event | category | flops | bytes accessed | tf_op | source)
XLA Modules:
  0.0 370.2 jit_solution(3389973030922674551)
XLA Ops:
  0.6 58.5 %shard_map.312 = (bf16[1024,1024]{1,0:T(8,128)(2,1)}, bf16[2,16,6144]{2,1,0:T(8,128)(2,1)}, bf16[16,4224]{1,0:T(8,128)(2,1)}, f32[2,1,3584]{2,1,0:T(1,128)}, bf1...) custom-call(bf16[2,1024,1024]{2,1,0:T(8,128)(2,1)} %tokens_ref.1, ...), custom_call_target="tpu_custom_call" | custom-call | flops 6442450944 | bytes 104857600 | tf_op jit(solution)/shard_map/pallas_call | solution.py:1069
  59.2 71.7 %shard_map.313 = (bf16[2048,512]{1,0:T(8,128)(2,1)}, f32[2048,512]{1,0:T(8,128)}, bf16[8,2048,2048]{2,1,0:T(8,128)(2,1)}, bf16[1024,512]{1,0:T(8,128)(2,1)}, bf1...) custom-call(bf16[2048,512]{1,0:T(8,128)(2,1)} %get-tuple-element.44., ...), custom_call_target="tpu_custom_call", output_to_operand_aliasing={{5}: (7, {}), {6}: (8, {}), {7}: (9, {})} | custom-call | flops 34359738368 | bytes 67108864 | tf_op jit(solution)/shard_map/pallas_call | solution.py:1315
  130.9 88.7 %shard_map.314 = (bf16[1024,1024]{1,0:T(8,128)(2,1)}, f32[1024,1024]{1,0:T(8,128)}, f32[2,16,4608]{2,1,0:T(8,128)}, f32[16,3072]{1,0:T(8,128)}, bf16[2048,512]{1...) custom-call(bf16[1024,1024]{1,0:T(8,128)(2,1)} %get-tuple-element.52, ...), custom_call_target="tpu_custom_call", output_to_operand_aliasing={{5}: (12, {}), {6}: (13, {})} | custom-call | flops 38654705664 | bytes 41943040 | tf_op jit(solution)/shard_map/pallas_call | solution.py:1803
  219.6 1.2 slice.27.tag_ref
  220.8 88.4 %shard_map.315 = (bf16[3,1024,512]{2,1,0:T(8,128)(2,1)}, bf16[3,1024,512]{2,1,0:T(8,128)(2,1)}, f32[8,16,7680]{2,1,0:T(8,128)}, bf16[2,1024,1024]{2,1,0:T(8,128)(2,1)}) custom-call(bf16[2048,512]{1,0:T(8,128)(2,1)} %get-tuple-element.44.q_ref, bf16[2048,512]{1,0:T(8,128)(2,1)} %get-tuple-element.45.k_ref, bf16[2048,512]{1,0:T(8,128)(2,1)} %get-tuple-element.46.v_ref, ...), custom_call_target="tpu_custom_call" | custom-call | flops 42949672960 | bytes 67108864 | tf_op jit(solution)/shard_map/pallas_call | solution.py:1534
  309.3 0.0 copy-start.1
  309.3 50.5 %shard_map.316 = (bf16[2,512,1024]{2,1,0:T(8,128)(2,1)}, f32[8,16,2560]{2,1,0:T(8,128)}) custom-call(bf16[1024,1024]{1,0:T(8,128)(2,1)} %get-tuple-element.52.x_ref, f32[1024,1024]{1,0:T(8,128)} %get-tuple-element.69.gh_ref, bf16[1024,1024]{1,0:T(8,128)(2,1)} %get-tuple-element.70.xn_ref, bf16[1024,16]{1,0:T(8,128)(2,1)} %get-tuple-element.71.u_ref, ...), custom_call_target="tpu_custom_call" | custom-call | flops 6442450944 | bytes 20971520 | tf_op jit(solution)/shard_map/pallas_call | solution.py:1962
  359.8 0.0 copy-start.3
  359.8 0.0 copy-done.1
  359.8 2.5 fusion
  362.3 0.0 copy-done.3
  362.3 0.0 copy-start
  362.3 0.1 slice.29
  362.4 0.9 copy.44
  363.3 1.5 slice_bitcast_fusion
  364.9 0.7 slice_bitcast_fusion.3
  365.6 0.0 copy-done
  365.6 0.0 copy-start.2
  365.6 2.1 copy.52
  367.7 1.0 copy-done.2
  368.7 1.3 copy.53
Async XLA Ops:
  309.3 50.5 %copy-start.1 = (f32[8,16,7680]{2,1,0:T(8,128)S(1)}, f32[8,16,7680]{2,1,0:T(8,128)}, u32[]{:S(2)}) copy-start(f32[8,16,7680]{2,1,0:T(8,128)} %get-tuple-element.77) | copy-start | bytes 11796484
  359.8 2.5 copy-start.3
  362.3 3.2 copy-start
  365.6 3.1 copy-start.2
where the time goes:
time: 373 us; the launch traced here: 370 us
  Pallas kernels  358 us (96%)
  local copies, waits for them, and re-layouts  11.4 us (3%)
    pallas_call x1, Pallas kernels, middle(): pl.pallas_call(functools.partial(middle_body, planes, blocks), grid=(2 *...  88.7 us
    pallas_call x1, Pallas kernels, attend_back(): pl.pallas_call(functools.partial(attend_back_body, planes), grid=(pairs,...  88.4 us
    pallas_call x1, Pallas kernels, attend(): pl.pallas_call(functools.partial(attend_body, planes, blocks), grid=(pair...  71.7 us
    pallas_call x1, Pallas kernels, project(): pl.pallas_call(functools.partial(project_body, planes, blocks), in_specs=...  58.5 us
    pallas_call x1, Pallas kernels, unproject(): pl.pallas_call(functools.partial(unproject_body, planes), in_specs=[hbm,...  50.5 us

commit v1 on v0

--- a/solution.py
+++ b/solution.py
@@ -568,7 +568,7 @@
 
 PROJECT_KINDS = (ALONG_Z, ALONG_Z)
 ATTEND_KINDS = (EVERY, ALONG_Z + TO_TP + TO_CORE, ALONG_Z + TO_CORE, ALONG_Z)
-MIDDLE_KINDS = ((), TO_TP + TO_NEXT, TO_TP + TO_NEXT, EVERY)
+MIDDLE_KINDS = ((), TO_NEXT, TO_TP + TO_NEXT, EVERY)
 
 
 def turned_copy(at, source, target, sems):
@@ -1213,6 +1213,9 @@
             flow.pass_on(2, z=True, core=True, wait=True)
         for flow in flows[3]:
             flow.pass_on(0, z=True)
+        for flow in flows[1]:
+            flow.pass_on(2, tp=True)
+            flow.pass_on(3, tp=True)
         for flow in zero:
             flow.pass_next(2)
             flow.pass_next(3)
@@ -1277,11 +1280,11 @@
                 flow.wait(NEXT_CAME, far)
                 flow.sent_next(far)
         for flow in flows[1]:
-            for far in range(2):
+            for far in range(planes):
                 flow.wait(TP_CAME, far)
         for flow in zero + flows[1]:
             for far in range(planes):
-                flow.sent(far, z=0 < far < last, tp=flow in zero or far < 2, core=True)
+                flow.sent(far, z=0 < far < last, tp=True, core=True)
         for flow in flows[2]:
             for far in range(planes):
                 flow.sent(far, z=far < last, core=True)
@@ -1633,10 +1636,8 @@
             flow.pass_on(1, fresh=False, z=True, core=True)
             flow.pass_on(0, fresh=False, core=True)
         for flow in flows[1]:
-            flow.pass_on(2, fresh=False, tp=True)
-            flow.pass_on(3, fresh=False, tp=True)
-            flow.pass_next(0, False)
-            flow.pass_next(1, False)
+            for far in planes_all:
+                flow.pass_next(far, False)
         pass_on(flows[2], tp=True)
         w_own, w_other = wo_half(core), wo_half(1 - core)
         for begin in range(0, rows_all, step):
@@ -1673,23 +1674,22 @@
         pass_on(flows[3], tp=True)
         arrived(flows[3], OWN_CAME)
 
-    @pl.when(f == 3)
-    def _():
-        for flow in flows[1]:
-            flow.pass_next(2)
-            flow.pass_next(3)
-
     @pl.when(f == 4)
     def _():
+        pass_next(flows[2], True)
         arrived(flows[1], NEXT_CAME)
 
     @pl.when(f == last - 2)
     def _():
-        pass_next(flows[2], True)
+        arrived(flows[2], NEXT_CAME)
+
+    @pl.when(f == last - 1)
+    def _():
+        pass_next(flows[3], True)
 
     slot = f % 2
 
-    @pl.when(f < last - 2)
+    @pl.when(f < last - 1)
     def _():
         for load in loads(f + 1, 1 - slot):
             load.start()
@@ -1722,17 +1722,9 @@
     t_split[tp_half, :, block_of(half + hidden_half)] = sum_rd
     t_split[tp_half, :, block_of(half)] = sum_eu
 
-    @pl.when(f == last - 2)
-    def _():
-        arrived(flows[2], NEXT_CAME)
-
     @pl.when(f == last - 1)
     def _():
-        pass_next(flows[3], True)
         arrived(flows[3], NEXT_CAME)
-
-    @pl.when((f == last - 2) | (f == last - 1))
-    def _():
         for load in loads(f + 1, 1 - slot):
             load.start()
 
@@ -1779,7 +1771,7 @@
         for index, pair in enumerate(flows[1:]):
             for flow in pair:
                 for far in planes_all:
-                    flow.sent(far, z=index == 2 and far in (1, 2), tp=index > 0 or far > 1, core=index == 2)
+                    flow.sent(far, z=index == 2 and far in (1, 2), tp=index > 0, core=index == 2)
                     flow.sent_next(far)
         for move in moves:
             move.wait()
@@ -1902,7 +1894,8 @@
             (jnp.logical_not(mine) & at.crosses, lambda: remote(both, 2), False),
         )
 
-    stages = [spread.second, spread.third, lambda: spread.planes(0), lambda: spread.planes(1)]
+    spread.second()
+    stages = [spread.third, lambda: spread.planes(0), lambda: spread.planes(1), lambda: spread.planes(2)]
     for count, i in enumerate(order):
         span = pl.ds(i * ROWS, ROWS)
         gx = dot(g1_vm[span, :], shared_ref[:, 0:width])
@@ -1914,7 +1907,7 @@
         for there, move, _ in moves(i):
             pl.when(there)(lambda move=move: move().start())
         stages[count]()
-    for distance in range(2, planes):
+    for distance in range(3, planes):
         spread.planes(distance)
     spread.finish()
     spread.sent()

time: 373 us -> 363 us (0.973)
  Pallas kernels: 358 us -> 348 us
    pallas_call x1, Pallas kernels: 88.7 us -> 82.7 us  [middle(): pl.pallas_call(functools.partial(middle_body, planes, blocks), grid=(2 *...]
    pallas_call x1, Pallas kernels: 50.5 us -> 46.8 us  [unproject(): pl.pallas_call(functools.partial(unproject_body, planes), in_specs=[hbm,...]
where the time goes in v1:
time: 363 us; the launch traced here: 361 us
  Pallas kernels  348 us (96%)
  local copies, waits for them, and re-layouts  11.4 us (3%)
    pallas_call x1, Pallas kernels, attend_back(): pl.pallas_call(functools.partial(attend_back_body, planes), grid=(pairs,...  88.4 us
    pallas_call x1, Pallas kernels, middle(): pl.pallas_call(functools.partial(middle_body, planes, blocks), grid=(2 *...  82.7 us
    pallas_call x1, Pallas kernels, attend(): pl.pallas_call(functools.partial(attend_body, planes, blocks), grid=(pair...  71.8 us
    pallas_call x1, Pallas kernels, project(): pl.pallas_call(functools.partial(project_body, planes, blocks), in_specs=...  58.5 us
    pallas_call x1, Pallas kernels, unproject(): pl.pallas_call(functools.partial(unproject_body, planes), in_specs=[hbm,...  46.8 us

profile of v1, /device:TPU:0, one launch (start us, length us, event | category | flops | bytes accessed | tf_op | source)
XLA Modules:
  0.0 360.5 jit_solution(10881308470339021013)
XLA Ops:
  0.6 58.5 %shard_map.312 = (bf16[1024,1024]{1,0:T(8,128)(2,1)}, bf16[2,16,6144]{2,1,0:T(8,128)(2,1)}, bf16[16,4224]{1,0:T(8,128)(2,1)}, f32[2,1,3584]{2,1,0:T(1,128)}, bf1...) custom-call(bf16[2,1024,1024]{2,1,0:T(8,128)(2,1)} %tokens_ref.1, ...), custom_call_target="tpu_custom_call" | custom-call | flops 6442450944 | bytes 104857600 | tf_op jit(solution)/shard_map/pallas_call | solution.py:1069
  59.2 71.8 %shard_map.313 = (bf16[2048,512]{1,0:T(8,128)(2,1)}, f32[2048,512]{1,0:T(8,128)}, bf16[8,2048,2048]{2,1,0:T(8,128)(2,1)}, bf16[1024,512]{1,0:T(8,128)(2,1)}, bf1...) custom-call(bf16[2048,512]{1,0:T(8,128)(2,1)} %get-tuple-element.44., ...), custom_call_target="tpu_custom_call", output_to_operand_aliasing={{5}: (7, {}), {6}: (8, {}), {7}: (9, {})} | custom-call | flops 34359738368 | bytes 67108864 | tf_op jit(solution)/shard_map/pallas_call | solution.py:1318
  130.9 82.7 %shard_map.314 = (bf16[1024,1024]{1,0:T(8,128)(2,1)}, f32[1024,1024]{1,0:T(8,128)}, f32[2,16,4608]{2,1,0:T(8,128)}, f32[16,3072]{1,0:T(8,128)}, bf16[2048,512]{1...) custom-call(bf16[1024,1024]{1,0:T(8,128)(2,1)} %get-tuple-element.52, ...), custom_call_target="tpu_custom_call", output_to_operand_aliasing={{5}: (12, {}), {6}: (13, {})} | custom-call | flops 38654705664 | bytes 41943040 | tf_op jit(solution)/shard_map/pallas_call | solution.py:1795
  213.7 1.2 slice.27.tag_ref
  214.9 88.4 %shard_map.315 = (bf16[3,1024,512]{2,1,0:T(8,128)(2,1)}, bf16[3,1024,512]{2,1,0:T(8,128)(2,1)}, f32[8,16,7680]{2,1,0:T(8,128)}, bf16[2,1024,1024]{2,1,0:T(8,128)(2,1)}) custom-call(bf16[2048,512]{1,0:T(8,128)(2,1)} %get-tuple-element.44.q_ref, bf16[2048,512]{1,0:T(8,128)(2,1)} %get-tuple-element.45.k_ref, bf16[2048,512]{1,0:T(8,128)(2,1)} %get-tuple-element.46.v_ref, ...), custom_call_target="tpu_custom_call" | custom-call | flops 42949672960 | bytes 67108864 | tf_op jit(solution)/shard_map/pallas_call | solution.py:1537
  303.4 0.0 copy-start.1
  303.4 46.8 %shard_map.316 = (bf16[2,512,1024]{2,1,0:T(8,128)(2,1)}, f32[8,16,2560]{2,1,0:T(8,128)}) custom-call(bf16[1024,1024]{1,0:T(8,128)(2,1)} %get-tuple-element.52.x_ref, f32[1024,1024]{1,0:T(8,128)} %get-tuple-element.69.gh_ref, bf16[1024,1024]{1,0:T(8,128)(2,1)} %get-tuple-element.70.xn_ref, bf16[1024,16]{1,0:T(8,128)(2,1)} %get-tuple-element.71.u_ref, ...), custom_call_target="tpu_custom_call" | custom-call | flops 6442450944 | bytes 20971520 | tf_op jit(solution)/shard_map/pallas_call | solution.py:1955
  350.1 0.0 copy-start.3
  350.1 0.0 copy-done.1
  350.1 2.5 fusion
  352.7 0.0 copy-done.3
  352.7 0.0 copy-start
  352.7 0.1 slice.29
  352.7 0.9 copy.44
  353.7 1.5 slice_bitcast_fusion
  355.2 0.7 slice_bitcast_fusion.3
  355.9 0.0 copy-done
  355.9 0.0 copy-start.2
  355.9 2.1 copy.52
  358.0 1.0 copy-done.2
  359.0 1.3 copy.53
Async XLA Ops:
  303.4 46.8 %copy-start.1 = (f32[8,16,7680]{2,1,0:T(8,128)S(1)}, f32[8,16,7680]{2,1,0:T(8,128)}, u32[]{:S(2)}) copy-start(f32[8,16,7680]{2,1,0:T(8,128)} %get-tuple-element.77) | copy-start | bytes 11796484
  350.1 2.5 copy-start.3
  352.7 3.2 copy-start
  355.9 3.1 copy-start.2

commit v2 on v1

--- a/solution.py
+++ b/solution.py
@@ -1386,7 +1386,6 @@
         pl.when(stays)(lambda: out_load.start())
         at.greet(True, True, True)
         spread.start()
-        pl.when(at.crosses)(lambda: out_turn.start())
 
     when(2, spread.second)
 
@@ -1399,9 +1398,14 @@
             out_tp(out_vm).start()
 
     when(4, spread.third)
+
+    @pl.when(now == 5)
+    def _():
+        pl.when(at.crosses)(lambda: out_turn.start())
+
     when(6, lambda: spread.planes(0))
 
-    @pl.when(now == 7)
+    @pl.when(now == 11)
     def _():
         @pl.when(at.crosses)
         def _():

time: 363 us -> 362 us (level)
  no operation moved by 1% of the time
where the time goes in v2:
time: 362 us; the launch traced here: 359 us
  Pallas kernels  346 us (96%)
  local copies, waits for them, and re-layouts  11.4 us (3%)
    pallas_call x1, Pallas kernels, attend_back(): pl.pallas_call(functools.partial(attend_back_body, planes), grid=(pairs,...  85.6 us
    pallas_call x1, Pallas kernels, middle(): pl.pallas_call(functools.partial(middle_body, planes, blocks), grid=(2 *...  82.7 us
    pallas_call x1, Pallas kernels, attend(): pl.pallas_call(functools.partial(attend_body, planes, blocks), grid=(pair...  71.8 us
    pallas_call x1, Pallas kernels, project(): pl.pallas_call(functools.partial(project_body, planes, blocks), in_specs=...  58.5 us
    pallas_call x1, Pallas kernels, unproject(): pl.pallas_call(functools.partial(unproject_body, planes), in_specs=[hbm,...  47.9 us

profile of v2, /device:TPU:0, one launch (start us, length us, event | category | flops | bytes accessed | tf_op | source)
XLA Modules:
  0.0 358.8 jit_solution(3884658804985146521)
XLA Ops:
  0.6 58.5 %shard_map.312 = (bf16[1024,1024]{1,0:T(8,128)(2,1)}, bf16[2,16,6144]{2,1,0:T(8,128)(2,1)}, bf16[16,4224]{1,0:T(8,128)(2,1)}, f32[2,1,3584]{2,1,0:T(1,128)}, bf1...) custom-call(bf16[2,1024,1024]{2,1,0:T(8,128)(2,1)} %tokens_ref.1, ...), custom_call_target="tpu_custom_call" | custom-call | flops 6442450944 | bytes 104857600 | tf_op jit(solution)/shard_map/pallas_call | solution.py:1069
  59.2 71.8 %shard_map.313 = (bf16[2048,512]{1,0:T(8,128)(2,1)}, f32[2048,512]{1,0:T(8,128)}, bf16[8,2048,2048]{2,1,0:T(8,128)(2,1)}, bf16[1024,512]{1,0:T(8,128)(2,1)}, bf1...) custom-call(bf16[2048,512]{1,0:T(8,128)(2,1)} %get-tuple-element.44., ...), custom_call_target="tpu_custom_call", output_to_operand_aliasing={{5}: (7, {}), {6}: (8, {}), {7}: (9, {})} | custom-call | flops 34359738368 | bytes 67108864 | tf_op jit(solution)/shard_map/pallas_call | solution.py:1318
  130.9 82.7 %shard_map.314 = (bf16[1024,1024]{1,0:T(8,128)(2,1)}, f32[1024,1024]{1,0:T(8,128)}, f32[2,16,4608]{2,1,0:T(8,128)}, f32[16,3072]{1,0:T(8,128)}, bf16[2048,512]{1...) custom-call(bf16[1024,1024]{1,0:T(8,128)(2,1)} %get-tuple-element.52, ...), custom_call_target="tpu_custom_call", output_to_operand_aliasing={{5}: (12, {}), {6}: (13, {})} | custom-call | flops 38654705664 | bytes 41943040 | tf_op jit(solution)/shard_map/pallas_call | solution.py:1799
  213.7 1.2 slice.27.tag_ref
  214.9 85.6 %shard_map.315 = (bf16[3,1024,512]{2,1,0:T(8,128)(2,1)}, bf16[3,1024,512]{2,1,0:T(8,128)(2,1)}, f32[8,16,7680]{2,1,0:T(8,128)}, bf16[2,1024,1024]{2,1,0:T(8,128)(2,1)}) custom-call(bf16[2048,512]{1,0:T(8,128)(2,1)} %get-tuple-element.44.q_ref, bf16[2048,512]{1,0:T(8,128)(2,1)} %get-tuple-element.45.k_ref, bf16[2048,512]{1,0:T(8,128)(2,1)} %get-tuple-element.46.v_ref, ...), custom_call_target="tpu_custom_call" | custom-call | flops 42949672960 | bytes 67108864 | tf_op jit(solution)/shard_map/pallas_call | solution.py:1541
  300.6 0.0 copy-start.1
  300.6 47.9 %shard_map.316 = (bf16[2,512,1024]{2,1,0:T(8,128)(2,1)}, f32[8,16,2560]{2,1,0:T(8,128)}) custom-call(bf16[1024,1024]{1,0:T(8,128)(2,1)} %get-tuple-element.52.x_ref, f32[1024,1024]{1,0:T(8,128)} %get-tuple-element.69.gh_ref, bf16[1024,1024]{1,0:T(8,128)(2,1)} %get-tuple-element.70.xn_ref, bf16[1024,16]{1,0:T(8,128)(2,1)} %get-tuple-element.71.u_ref, ...), custom_call_target="tpu_custom_call" | custom-call | flops 6442450944 | bytes 20971520 | tf_op jit(solution)/shard_map/pallas_call | solution.py:1959
  348.4 0.0 copy-start.3
  348.4 0.0 copy-done.1
  348.4 2.5 fusion
  351.0 0.0 copy-done.3
  351.0 0.0 copy-start
  351.0 0.1 slice.29
  351.0 0.9 copy.44
  352.0 1.5 slice_bitcast_fusion
  353.5 0.7 slice_bitcast_fusion.3
  354.2 0.0 copy-done
  354.2 0.0 copy-start.2
  354.2 2.1 copy.52
  356.3 1.0 copy-done.2
  357.3 1.3 copy.53
Async XLA Ops:
  300.6 47.9 %copy-start.1 = (f32[8,16,7680]{2,1,0:T(8,128)S(1)}, f32[8,16,7680]{2,1,0:T(8,128)}, u32[]{:S(2)}) copy-start(f32[8,16,7680]{2,1,0:T(8,128)} %get-tuple-element.77) | copy-start | bytes 11796484
  348.4 2.5 copy-start.3
  351.0 3.2 copy-start
  354.2 3.1 copy-start.2
